TPU v7x, 32 devices: a whole 2x2x4 slice. The times are simulated.
32 devices in a mesh: freq: 8 (over y, x, core), lat: 4 (over z).
Axes of the slice: x: 2, y: 2, z: 4, core: 2. Of those that a mesh axis runs over, the one named last changes fastest.
Arguments:
- record: float32 [8, 2, 4, 4096], P(None, None, 'lat', 'freq'), may hold values from -6 to 6
- receiver_cell: int32 [4, 4096], P('lat'), may hold values from 0 to 131071
- source_cell: int32 [1], replicated, may hold values from 0 to 524287
- wavelet: float32 [8, 2], P('freq'), may hold values from -4 to 4
- frequency_index: int32 [8], P('freq'), may hold values from 8 to 199
- slowness: float32 [2, 512, 1024], P(None, 'lat', 'freq'), may hold values from 0.000222 to 0.000667
- anisotropy: float32 [2, 512, 1024], P(None, 'lat', 'freq'), may hold values from 0.05 to 0.4
- reference_slowness: float32 [2], replicated, may hold values from 0.00025 to 0.00059
- reference_anisotropy: float32 [2], replicated, may hold values from 0.05 to 0.3
- correction_block: bfloat16 [2, 128, 128], replicated, may hold values from -0.31 to 1.61
Outputs:
- migrated_image: float32 [2, 512, 1024], P(None, 'lat', 'freq')
- wavefields: bfloat16 [2, 8, 2, 512, 1024], P(None, 'freq', None, 'lat')
All inputs are finite; a program needn't handle non-finite values.
Results may differ from a plain program's by a relative error of at most 0.034.
Values may be sent and summed in bfloat16 or wider, within the bound.
A program may use at most 256 MiB of HBM per device.

v0:
```python
import math

import jax
import jax.numpy as jnp
from jax import lax
from jax.sharding import PartitionSpec as P

NX = 1024
NY = 512
STEPS = 2


grid_step = 10.0
depth_step = 10.0
freq_step = 0.25
datum_depth = 2000.0
water_slowness = 1.0 / 1500.0


def transform_table(length, direction):
    indices = jnp.arange(length, dtype=jnp.int32)
    products = indices[:, None] * indices[None, :] % length
    angles = products.astype(jnp.float32) * (2.0 * math.pi / length)
    factor = 1.0 / math.sqrt(length)
    cosine = jnp.cos(angles) * factor
    sine_part = direction * jnp.sin(angles) * factor
    top_rows = jnp.stack([cosine, sine_part], axis=1)
    low_rows = jnp.stack([-sine_part, cosine], axis=1)
    return jnp.stack([top_rows, low_rows], axis=0).astype(jnp.bfloat16)


def wavenumber(indices, length):
    signed = jnp.where(indices < length // 2, indices, indices - length)
    return signed.astype(jnp.float32) * (2.0 * math.pi / (length * grid_step))


def source_field(wavelet, angular, line_index, cell_index, source_cell, width):
    source_line = source_cell[0] // width
    source_col = source_cell[0] - source_line * width
    off_line = (line_index - source_line).astype(jnp.float32) * grid_step
    off_col = (cell_index - source_col).astype(jnp.float32) * grid_step
    radius = jnp.sqrt(off_line[:, None] ** 2 + off_col[None, :] ** 2 + datum_depth**2)
    amplitude = datum_depth / radius
    phase = angular[:, None, None] * (radius * water_slowness)[None]
    cosine = amplitude[None] * jnp.cos(phase)
    sine_part = amplitude[None] * jnp.sin(phase)
    wave_real = wavelet[:, 0][:, None, None]
    wave_imag = wavelet[:, 1][:, None, None]
    real_part = wave_real * cosine - wave_imag * sine_part
    imag_part = wave_real * sine_part + wave_imag * cosine
    return jnp.stack([real_part, imag_part], axis=1)


def rotate(wavefield, cosine, sine_part):
    field_sign = jnp.array([1.0, -1.0], jnp.float32).reshape(2, 1, 1, 1)
    signed_sine = sine_part[None] * field_sign
    real_part = wavefield[:, :, 0]
    imag_part = wavefield[:, :, 1]
    next_real = real_part * cosine[None] - imag_part * signed_sine
    next_imag = imag_part * cosine[None] + real_part * signed_sine
    return jnp.stack([next_real, next_imag], axis=2)


def propagate(spectrum, angular, wave_y, wave_x, slow_ref, aniso_ref):
    lateral = wave_y[:, None] ** 2 + wave_x[None, :] ** 2
    vertical = ((angular * slow_ref) ** 2)[:, None, None] - (1.0 + 2.0 * aniso_ref) * lateral[None]
    real_root = jnp.sqrt(jnp.maximum(vertical, 0.0))
    decay_root = jnp.sqrt(jnp.maximum(-vertical, 0.0))
    damping = jnp.exp(-decay_root * depth_step)
    return rotate(
        spectrum,
        damping * jnp.cos(real_root * depth_step),
        damping * jnp.sin(real_root * depth_step),
    )


def correct(space, angular, slow_now, aniso_now, slow_ref, block):
    phases = angular[:, None, None] * (slow_now - slow_ref)[None] * depth_step
    split = rotate(space, jnp.cos(phases), jnp.sin(phases)).astype(jnp.bfloat16)
    shape = split.shape
    width = block.shape[0]
    blocks = split.reshape(shape[:4] + (shape[4] // width, width))
    correction = jnp.einsum(
        "gfcajb,bd->gfcajd", blocks, block, preferred_element_type=jnp.float32
    ).reshape(shape)
    coefficient = angular[:, None, None] * (slow_now * aniso_now)[None] * depth_step
    field_sign = jnp.array([1.0, -1.0], jnp.float32).reshape(2, 1, 1, 1)
    scaled = coefficient[None] * field_sign
    base = split.astype(jnp.float32)
    next_real = base[:, :, 0] - scaled * correction[:, :, 1]
    next_imag = base[:, :, 1] + scaled * correction[:, :, 0]
    return jnp.stack([next_real, next_imag], axis=2).astype(jnp.bfloat16)


def body(
    record,
    receiver_cell,
    source_cell,
    wavelet,
    frequency_index,
    slowness,
    anisotropy,
    reference_slowness,
    reference_anisotropy,
    correction_block,
):
    lat_index = lax.axis_index("lat")
    slab_rows = slowness.shape[1]
    slab_cells = slab_rows * NX
    regrouped = lax.all_to_all(
        record.astype(jnp.bfloat16), "freq", split_axis=0, concat_axis=3, tiled=True
    ).astype(record.dtype)
    nfreqs = regrouped.shape[0]
    values = regrouped.reshape(nfreqs * 2, -1)
    targets = receiver_cell.reshape(-1)
    receiver = jnp.zeros((nfreqs * 2, slab_cells), jnp.float32).at[:, targets].add(values)
    receiver = receiver.reshape(nfreqs, 2, slab_rows, NX)
    angular = frequency_index.astype(jnp.float32) * (2.0 * math.pi * freq_step)
    own_lines = lat_index * slab_rows + jnp.arange(slab_rows, dtype=jnp.int32)
    source = source_field(
        wavelet, angular, own_lines, jnp.arange(NX, dtype=jnp.int32), source_cell, NX
    )
    wavefield = jnp.stack([source, receiver]).astype(jnp.bfloat16)
    forward_x = transform_table(NX, -1.0)
    inverse_x = transform_table(NX, 1.0)
    forward_y = transform_table(NY, -1.0)
    inverse_y = transform_table(NY, 1.0)
    image_parts = []
    for depth_index in range(STEPS):
        slow_now, aniso_now = (
            lax.all_gather(
                slowness[depth_index].astype(jnp.bfloat16), "freq", axis=1, tiled=True
            ).astype(jnp.float32),
            lax.all_gather(
                anisotropy[depth_index].astype(jnp.bfloat16), "freq", axis=1, tiled=True
            ).astype(jnp.float32),
        )
        slow_ref = reference_slowness[depth_index]
        aniso_ref = reference_anisotropy[depth_index]
        x_spectrum = jnp.einsum(
            "gfcyx,cxdk->gfdyk", wavefield, forward_x, preferred_element_type=jnp.float32
        ).astype(jnp.bfloat16)
        columns = lax.all_to_all(x_spectrum, "lat", split_axis=4, concat_axis=3, tiled=True)
        col_width = columns.shape[4]
        spectrum = jnp.einsum(
            "gfcyx,cydk->gfdkx", columns, forward_y, preferred_element_type=jnp.float32
        )
        wave_x = wavenumber(lat_index * col_width + jnp.arange(col_width, dtype=jnp.int32), NX)
        wave_y = wavenumber(jnp.arange(NY, dtype=jnp.int32), NY)
        shifted = propagate(spectrum, angular, wave_y, wave_x, slow_ref, aniso_ref).astype(
            jnp.bfloat16
        )
        back_cols = jnp.einsum(
            "gfcyx,cydk->gfdkx", shifted, inverse_y, preferred_element_type=jnp.float32
        ).astype(jnp.bfloat16)
        back_rows = lax.all_to_all(back_cols, "lat", split_axis=3, concat_axis=4, tiled=True)
        space = jnp.einsum(
            "gfcyx,cxdk->gfdyk", back_rows, inverse_x, preferred_element_type=jnp.float32
        )
        wavefield = correct(
            space, angular, slow_now, aniso_now, slow_ref, correction_block[depth_index]
        )
        wide = wavefield.astype(jnp.float32)
        imaging = jnp.sum(wide[0, :, 0] * wide[1, :, 0] + wide[0, :, 1] * wide[1, :, 1], axis=0)
        image_parts.append(
            lax.psum_scatter(
                imaging.astype(jnp.bfloat16), "freq", scatter_dimension=1, tiled=True
            ).astype(jnp.float32)
        )
    migrated = jnp.stack(image_parts)
    return (migrated, wavefield)


def solution(mesh):
    return jax.shard_map(
        body,
        mesh=mesh,
        in_specs=(
            P(None, None, "lat", "freq"),
            P("lat", None),
            P(),
            P("freq", None),
            P("freq"),
            P(None, "lat", "freq"),
            P(None, "lat", "freq"),
            P(),
            P(),
            P(),
        ),
        out_specs=(P(None, "lat", "freq"), P(None, "freq", None, "lat", None)),
        check_vma=False,
    )
```

profile of v0, /device:TPU:0, one launch (start us, length us, event | category | flops | bytes accessed | tf_op | source)
XLA Modules:
  0.0 465.4 jit_solution(8514137938401349631)
XLA Ops:
  8.6 5.2 %all-to-all-start = ((bf16[8,2,512]{2,1,0:T(2,128)(2,1)}), bf16[8,2,512]{2,1,0:T(2,128)(2,1)S(1)}, u32[]{:S(2)}, u32[]{:S(2)}) async-start(bf16[8,2,512]{2,1,0:T(2,128)(2,1)} %bitcast.279), calls=%async_computation | async-start | bytes 32768 | tf_op jit(solution)/shard_map/all_to_all | solution.py:110
  13.7 16.8 %negate_convert_fusion = (bf16[1024,1,1024]{0,2,1:T(8,128)(2,1)S(1)}, bf16[1024,1,1024]{0,2,1:T(8,128)(2,1)}) fusion(), kind=kLoop, calls=%fused_computation.29 | loop fusion | flops 20971520 | bytes 4194304 | tf_op jit(solution)/shard_map/convert.46
  30.5 18.0 %multiply_convert_fusion = (bf16[1024,1,1024]{0,2,1:T(8,128)(2,1)}, bf16[1024,1,1024]{0,2,1:T(8,128)(2,1)}) fusion(), kind=kLoop, calls=%fused_computation.31 | loop fusion | flops 18874368 | bytes 4194304 | tf_op jit(solution)/shard_map/convert.73
  48.5 16.5 %multiply_convert_fusion.2 = bf16[1024,1,1024]{0,2,1:T(8,128)(2,1)} fusion(), kind=kLoop, calls=%fused_computation.36 | loop fusion | flops 16777216 | bytes 2097152 | tf_op jit(solution)/shard_map/convert.74
  67.1 5.1 %sort = (s32[4096]{0:T(1024)S(1)}, s32[4096]{0:T(1024)S(1)}) sort(s32[4096]{0:T(1024)S(1)} %bitcast.305, s32[4096]{0:T(1024)S(1)} %iota.98), dimensions={0}, to_apply=%compare | sort | flops 49152 | bytes 65536 | tf_op jit(solution)/shard_map/scatter-add | solution.py:116
  72.2 3.9 subtract_convert_fusion
  76.1 10.1 %fusion.15 = (bf16[1,1024,2,1024]{1,3,0,2:T(8,128)(2,1)}, bf16[1,1024,2,1024]{1,3,0,2:T(8,128)(2,1)}, bf16[1,1024,2,1024]{1,3,2,0:T(8,128)(2,1)}, bf16[1,1024,2,1024]{1,3,2,0:T(8,128)(2,1)}) fusion(bf16[1024,1,1024]{0,2,1:T(8,128)(2,1)} %get-tuple-element.56, bf16[1024,1,1024]{0,2,1:T(8,128)(2,1)} %get-tuple-element.57, ...), kind=kLoop, calls=%fused_computation.25 | loop fusion | flops 8388608 | bytes 27262976 | tf_op jit(solution)/shard_map/stack | solution.py:29
  87.0 69.0 %scatter_custom_fusion = f32[2,131072]{0,1:T(8,128)} fusion(s32[4096]{0:T(1024)S(1)} %get-tuple-element.10, f32[]{:T(128)} %constant.103.clone.1, f32[4096,2]{1,0:T(8,128)S(1)} %copy.140, s32[4096]{0:T(1024)S(1)} %broadcast_clamp_fusion), kind=kCustom, calls=%fused_computation.2 | custom fusion | flops 8192 | bytes 1048580 | tf_op jit(solution)/shard_map/scatter-add | solution.py:116
  156.0 32.5 %convert.170 = bf16[2,131072]{0,1:T(8,128)(2,1)} convert(f32[2,131072]{0,1:T(8,128)} %scatter_custom_fusion) | non-fusion elementwise | flops 262144 | bytes 1572864 | tf_op jit(solution)/shard_map/convert.40
  188.4 23.7 %copy.212 = bf16[2,131072]{1,0:T(2,128)(2,1)S(1)} copy(bf16[2,131072]{0,1:T(8,128)(2,1)} %convert.170) | data formatting | bytes 1048576
  212.3 5.9 %fusion.44 = bf16[2,1,2,128,1024]{3,4,0,2,1:T(8,128)(2,1)S(1)} fusion(bf16[1,1024,2,1024]{1,3,0,2:T(8,128)(2,1)} %get-tuple-element.23, bf16[1,1024,2,1024]{1,3,0,2:T(8,128)(2,1)} %get-tuple-element.22, bf16[1,2,128,1024]{3,2,1,0:T(8,128)(2,1)S(1)} %copy.249, bf16[1,1,128,1024]{3,2,1,0:T(8,128)(2,1)S(1)} %get-tuple-element.43, ...), kind=kOutput, calls=%fused_computation.68 | convolution fusion | flops 2167930880 | bytes 10485760 | tf_op jit(solution)/shard_map/gfcyx,cxdk->gfdyk/dot_general | solution.py:140
  220.2 4.9 %all-to-all-start.1 = ((bf16[2,1,2,128,1024]{3,0,2,1,4:T(2,128)(2,1)}), bf16[2,1,2,128,1024]{3,0,2,1,4:T(2,128)(2,1)S(1)}, u32[]{:S(2)}, u32[]{:S(2)}) async-start(bf16[2,1,2,128,1024]{3,0,2,1,4:T(2,128)(2,1)} %copy.142), calls=%async_computation.1 | async-start | bytes 2097152 | tf_op jit(solution)/shard_map/all_to_all | solution.py:143
  228.9 4.0 multiply_convert_fusion.5
  232.9 4.0 negate_convert_fusion.2
  237.0 4.4 multiply_convert_fusion.3
  243.1 6.1 %fusion.156 = (f32[512,256]{1,0:T(8,128)}, f32[512,256]{1,0:T(8,128)}, f32[512,256]{1,0:T(8,128)}, f32[512,256]{1,0:T(8,128)}) fusion(f32[]{:T(128)} %bitcast.93, f32[]{:T(128)} %bitcast.92, f32[256]{0:T(256)S(1)} %fusion.180, f32[512]{0:T(512)S(1)} %fusion.177, f32[]{:T(128)} %bitcast.39, f32[]{:T(128)} %bitcast.38), kind=kLoop, calls=%fused_computation.200 | loop fusion | flops 2752512 | bytes 2100240 | tf_op jit(solution)/shard_map/mul | solution.py:72
  253.0 2.9 convolution_bitcast_fusion.1
  259.9 3.5 all-to-all-start.2
  263.5 9.7 %all-gather = bf16[1,128,1024]{2,1,0:T(8,128)(2,1)S(1)} all-gather(bf16[1,128,128]{2,1,0:T(8,128)(2,1)S(1)} %get-tuple-element.41), channel_id=2, replica_groups=mesh['freq'=8,'lat'=4] {'freq'}, dimensions={2}, use_global_device_ids=true | all-gather | bytes 294912 | tf_op jit(solution)/shard_map/all_gather | solution.py:131
  273.2 9.3 %all-gather.1 = bf16[1,128,1024]{2,1,0:T(8,128)(2,1)S(1)} all-gather(bf16[1,128,128]{2,1,0:T(8,128)(2,1)S(1)} %get-tuple-element.39), channel_id=3, replica_groups=mesh['freq'=8,'lat'=4] {'freq'}, dimensions={2}, use_global_device_ids=true | all-gather | bytes 294912 | tf_op jit(solution)/shard_map/all_gather | solution.py:134
  282.5 8.4 %all-gather.2 = bf16[1,128,1024]{2,1,0:T(8,128)(2,1)S(1)} all-gather(bf16[1,128,128]{2,1,0:T(8,128)(2,1)S(1)} %get-tuple-element.40), channel_id=4, replica_groups=mesh['freq'=8,'lat'=4] {'freq'}, dimensions={2}, use_global_device_ids=true | all-gather | bytes 294912 | tf_op jit(solution)/shard_map/all_gather | solution.py:131
  290.9 9.3 %all-gather.3 = bf16[1,128,1024]{2,1,0:T(8,128)(2,1)S(1)} all-gather(bf16[1,128,128]{2,1,0:T(8,128)(2,1)S(1)} %get-tuple-element.38), channel_id=5, replica_groups=mesh['freq'=8,'lat'=4] {'freq'}, dimensions={2}, use_global_device_ids=true | all-gather | bytes 294912 | tf_op jit(solution)/shard_map/all_gather | solution.py:134
  300.3 6.1 %fusion.114 = (f32[128,1024]{1,0:T(8,128)S(1)}, f32[128,1024]{1,0:T(8,128)S(1)}, f32[128,1024]{1,0:T(8,128)S(1)}, f32[128,1024]{1,0:T(8,128)}, f32[128,1024]{1,0:T(8,128)}, /*index=5*/f32[128,1024]{1,0:T(8,128)}) fusion(bf16[1,128,1024]{2,1,0:T(8,128)(2,1)S(1)} %all-gather, bf16[1,128,1024]{2,1,0:T(8,128)(2,1)S(1)} %all-gather.1, f32[]{:T(128)} %bitcast.18, ...), kind=kLoop, calls=%fused_computation.158 | loop fusion | flops 2097152 | bytes 4194316 | tf_op jit(solution)/shard_map/mul | solution.py:86
  306.9 9.4 %fusion.188 = (bf16[2,1024,2,1024,1]{1,3,2,0,4:T(8,128)(2,1)}, bf16[2,1024,2,1024]{1,3,2,0:T(8,128)(2,1)}) fusion(bf16[1,1024,2,1024]{1,3,2,0:T(8,128)(2,1)} %get-tuple-element.24, bf16[1,1024,2,1024]{1,3,2,0:T(8,128)(2,1)} %get-tuple-element.25), kind=kLoop, calls=%fused_computation.251 | loop fusion | flops 4194304 | bytes 25165824 | tf_op jit(solution)/shard_map/stack | solution.py:29
  319.9 4.8 %fusion.30 = f32[2,1,2,128,1024]{3,4,0,2,1:T(8,128)S(1)} fusion(bf16[2,2,128,1024,1]{3,2,1,0,4:T(8,128)(2,1)S(1)} %reshape.1181, bf16[2,1024,2,1024,1]{1,3,2,0,4:T(8,128)(2,1)} %get-tuple-element.12), kind=kOutput, calls=%fused_computation.49 | convolution fusion | flops 2147483648 | bytes 11534336 | tf_op jit(solution)/shard_map/gfcyx,cxdk->gfdyk/dot_general | solution.py:157
  333.6 2.4 fusion.47
  337.1 31.3 %all_to_all.69 = bf16[2,1,2,128,1024]{3,0,2,1,4:T(2,128)(2,1)S(1)} all-to-all(bf16[2,1,2,128,1024]{3,0,2,1,4:T(2,128)(2,1)S(1)} %copy.164), channel_id=1, replica_groups=mesh['freq'=8,'lat'=4] {'lat'}, dimensions={4} | all-to-all | bytes 2097152 | tf_op jit(solution)/shard_map/all_to_all | solution.py:143
  370.0 2.9 convolution_bitcast_fusion
  376.8 3.5 all-to-all-start.4
  385.5 20.2 %all-to-all-done.4 = bf16[2,1,2,512,256]{4,0,2,1,3:T(2,128)(2,1)S(1)} async-done(((bf16[2,1,2,512,256]{4,0,2,1,3:T(2,128)(2,1)}), bf16[2,1,2,512,256]{4,0,2,1,3:T(2,128)(2,1)S(1)}, u32[]{:S(2)}, u32[]{:S(2)}) %all-to-all-start.4) | async-done | bytes 1048608 | tf_op jit(solution)/shard_map/all_to_all | solution.py:156
  407.3 4.9 %fusion.33 = f32[2,1,2,128,1024]{3,4,2,1,0:T(8,128)S(1)} fusion(bf16[2,1024,2,1024]{1,3,2,0:T(8,128)(2,1)} %get-tuple-element.13, bf16[2,2,128,1024,1]{3,2,1,0,4:T(8,128)(2,1)S(1)} %reshape.1192), kind=kOutput, calls=%fused_computation.50 | convolution fusion | flops 2147483648 | bytes 11534336 | tf_op jit(solution)/shard_map/gfcyx,cxdk->gfdyk/dot_general | solution.py:157
  419.6 36.9 %reduce-scatter.5.cloned.1.call-done = bf16[128,128]{0,1:T(8,128)(2,1)} async-done(((bf16[128,1024]{0,1:T(8,128)(2,1)}), bf16[128,128]{0,1:T(8,128)(2,1)}) %reduce-scatter.5.cloned.1.call-update) | async-done | bytes 32784 | tf_op jit(solution)/shard_map/reduce_scatter | solution.py:166
  (122 shorter events, 50.5 us)
Async XLA Ops:
  8.6 77.6 %all-to-all-start = ((bf16[8,2,512]{2,1,0:T(2,128)(2,1)}), bf16[8,2,512]{2,1,0:T(2,128)(2,1)S(1)}, u32[]{:S(2)}, u32[]{:S(2)}) async-start(bf16[8,2,512]{2,1,0:T(2,128)(2,1)} %bitcast.279), calls=%async_computation | async-start | bytes 32768 | tf_op jit(solution)/shard_map/all_to_all | solution.py:110
  30.5 35.9 %copy-start.22 = (f32[1,2]{1,0:T(1,128)S(1)}, f32[1,2]{1,0:T(1,128)}, u32[]{:S(2)}) copy-start(f32[1,2]{1,0:T(1,128)} %param.19) | copy-start | bytes 28
  30.5 36.5 %copy-start.21 = (s32[1,4096]{1,0:T(1,128)S(1)}, s32[1,4096]{1,0:T(1,128)}, u32[]{:S(2)}) copy-start(s32[1,4096]{1,0:T(1,128)} %param.17) | copy-start | bytes 49156
  218.1 7.0 %copy-start.23 = (f32[2]{0:T(128)S(1)}, f32[2]{0:T(128)}, u32[]{:S(2)}) copy-start(f32[2]{0:T(128)} %param.23) | copy-start | bytes 28
  218.1 8.8 %copy-start.24 = (f32[2]{0:T(128)S(1)}, f32[2]{0:T(128)}, u32[]{:S(2)}) copy-start(f32[2]{0:T(128)} %param.24) | copy-start | bytes 28
  220.2 31.3 %all-to-all-start.1 = ((bf16[2,1,2,128,1024]{3,0,2,1,4:T(2,128)(2,1)}), bf16[2,1,2,128,1024]{3,0,2,1,4:T(2,128)(2,1)S(1)}, u32[]{:S(2)}, u32[]{:S(2)}) async-start(bf16[2,1,2,128,1024]{3,0,2,1,4:T(2,128)(2,1)} %copy.142), calls=%async_computation.1 | async-start | bytes 2097152 | tf_op jit(solution)/shard_map/all_to_all | solution.py:143
  243.1 13.4 %copy-start.9 = (bf16[1,512,2,512]{1,3,2,0:T(8,128)(2,1)}, bf16[1,512,2,512]{1,3,2,0:T(8,128)(2,1)S(1)}, u32[]{:S(2)}) copy-start(bf16[1,512,2,512]{1,3,2,0:T(8,128)(2,1)S(1)} %get-tuple-element.30) | copy-start | bytes 3145732
  253.0 3.0 copy-start.15
  253.0 3.0 copy-start.16
  253.0 3.0 copy-start.20
  253.0 3.5 copy-start.11
  257.8 5.6 %copy-start.17 = (f32[2,128,128]{2,1,0:T(8,128)S(1)}, f32[2,128,128]{2,1,0:T(8,128)}, u32[]{:S(2)}) copy-start(f32[2,128,128]{2,1,0:T(8,128)} %param.21) | copy-start | bytes 393220
  257.8 5.6 %copy-start.18 = (f32[2,128,128]{2,1,0:T(8,128)S(1)}, f32[2,128,128]{2,1,0:T(8,128)}, u32[]{:S(2)}) copy-start(f32[2,128,128]{2,1,0:T(8,128)} %param.22) | copy-start | bytes 393220
  259.9 56.5 %all-to-all-start.2 = ((bf16[2,1,2,512,256]{4,0,2,1,3:T(2,128)(2,1)}), bf16[2,1,2,512,256]{4,0,2,1,3:T(2,128)(2,1)S(1)}, u32[]{:S(2)}, u32[]{:S(2)}) async-start(bf16[2,1,2,512,256]{4,0,2,1,3:T(2,128)(2,1)} %copy.146), calls=%async_computation.2 | async-start | bytes 2097152 | tf_op jit(solution)/shard_map/all_to_all | solution.py:156
  326.1 3.5 copy-start.19
  329.6 2.5 copy-start
  329.6 4.0 copy-start.1
  332.0 4.0 copy-start.8
  369.9 3.0 copy-start.13
  369.9 3.0 copy-start.14
  369.9 3.5 copy-start.10
  370.0 3.5 copy-start.12
  374.7 5.7 %copy-start.4 = (f32[128,1024]{1,0:T(8,128)S(1)}, f32[128,1024]{1,0:T(8,128)}, u32[]{:S(2)}) copy-start(f32[128,1024]{1,0:T(8,128)} %get-tuple-element.63) | copy-start | bytes 1572868
  374.8 6.7 %copy-start.3 = (f32[128,1024]{1,0:T(8,128)S(1)}, f32[128,1024]{1,0:T(8,128)}, u32[]{:S(2)}) copy-start(f32[128,1024]{1,0:T(8,128)} %get-tuple-element.62) | copy-start | bytes 1572868
  374.8 7.7 %copy-start.2 = (f32[128,1024]{1,0:T(8,128)S(1)}, f32[128,1024]{1,0:T(8,128)}, u32[]{:S(2)}) copy-start(f32[128,1024]{1,0:T(8,128)} %get-tuple-element.64) | copy-start | bytes 1572868
  376.8 28.9 %all-to-all-start.4 = ((bf16[2,1,2,512,256]{4,0,2,1,3:T(2,128)(2,1)}), bf16[2,1,2,512,256]{4,0,2,1,3:T(2,128)(2,1)S(1)}, u32[]{:S(2)}, u32[]{:S(2)}) async-start(bf16[2,1,2,512,256]{4,0,2,1,3:T(2,128)(2,1)} %copy.168), calls=%async_computation.5 | async-start | bytes 2097152 | tf_op jit(solution)/shard_map/all_to_all | solution.py:156
  380.4 39.3 %reduce-scatter.3.cloned.1.call-start = ((), (), s32[]{:S(2)}) async-start(), calls=%async_computation.7 | async-start | bytes 294912 | tf_op jit(solution)/shard_map/reduce_scatter | solution.py:166
  385.5 71.1 %reduce-scatter.5.cloned.1.call-start = ((), (), s32[]{:S(2)}) async-start(), calls=%async_computation.8 | async-start | bytes 294912 | tf_op jit(solution)/shard_map/reduce_scatter | solution.py:166
  407.3 4.9 %copy-start.6 = (f32[128,1024]{0,1:T(8,128)S(1)}, f32[128,1024]{0,1:T(8,128)}, u32[]{:S(2)}) copy-start(f32[128,1024]{0,1:T(8,128)} %copy.172) | copy-start | bytes 1572868
  407.3 4.9 %copy-start.7 = (f32[128,1024]{0,1:T(8,128)S(1)}, f32[128,1024]{0,1:T(8,128)}, u32[]{:S(2)}) copy-start(f32[128,1024]{0,1:T(8,128)} %copy.173) | copy-start | bytes 1572868
  413.8 2.7 copy-start.5
Sparse Core Ops, SparseCore 0:
  385.6 33.9 reduce-scatter.2
  422.9 33.5 reduce-scatter.4
where the time goes:
time: 474 us; the launch traced here: 465 us
  other arithmetic  218 us (46%)
  blocking collectives  68.1 us (14%)
  waiting for transfers between devices  59.9 us (13%)
  local copies, waits for them, and re-layouts  53.7 us (11%)
  matrix products  29.9 us (6%)
  between operations  19 us (4%)
  starting transfers between devices  17.2 us (4%)
    another operation x17, other arithmetic  103 us
    scatter-add x3, other arithmetic, body(): jnp.zeros((nfreqs * 2, slab_cells), jnp.float32).at[:, targets].add(values)  74.1 us
    reduce_scatter x2, waiting for transfers between devices, body(): lax.psum_scatter(imaging.astype(jnp.bfloat16), 'freq', scatter_dimension=...  37.3 us
    all_to_all x1, blocking collectives, body(): lax.all_to_all(x_spectrum, 'lat', split_axis=4, concat_axis=3, tiled=True)  31.3 us
    unnamed x56, local copies, waits for them, and re-layouts  28.2 us
    another operation x3, other arithmetic, transform_table(): return jnp.stack([top_rows, low_rows], axis=0).astype(jnp.bfloat16)  21.3 us
    all_to_all x2, waiting for transfers between devices, body(): lax.all_to_all(back_cols, 'lat', split_axis=3, concat_axis=4, tiled=True)  20.2 us
    all_gather x2, blocking collectives, body(): lax.all_gather(anisotropy[depth_index].astype(jnp.bfloat16), 'freq', axis...  18.6 us
  transfers between devices with their start and end apart: 6, of which 4 were waited for; matrix products, arithmetic and copies ran while one was open for 27% of the time, Pallas kernels for 0%

commit v1 on v0

v1 whole, which is shorter than its diff:
```python
import functools
import math

import jax
import jax.numpy as jnp
import ml_dtypes
import numpy as np
from jax import lax
from jax.experimental import pallas as pl
from jax.experimental.pallas import tpu as pltpu
from jax.sharding import PartitionSpec as P

NX = 1024
NY = 512
STEPS = 2
SLAB = 128
TILE = 256
HALF = 512

grid_step = 10.0
depth_step = 10.0
freq_step = 0.25
datum_depth = 2000.0
water_slowness = 1.0 / 1500.0
f32 = jnp.float32
bf16 = jnp.bfloat16
VMEM_LIMIT = 50 * 1024 * 1024


def trig(length):
    idx = np.arange(length)
    ang = (idx[:, None] * idx[None, :] % length) * (2.0 * math.pi / length)
    return np.cos(ang) / math.sqrt(length), np.sin(ang) / math.sqrt(length)


def tables():
    cx, sx = trig(NX)
    xt = np.stack([cx, sx]).astype(ml_dtypes.bfloat16)
    cy, sy = trig(NY)
    rows = np.arange(NY).reshape(2, 2, SLAB)
    fwd = []
    for s in range(2):
        ys = rows[:, s].reshape(-1)
        c, e = cy[:, ys], -sy[:, ys]
        fwd.append(np.block([[c, -e], [e, c]]))
    inv = []
    for hi in range(2):
        per = []
        for s in range(2):
            c, e = cy[rows[hi, s]], sy[rows[hi, s]]
            per.append(np.block([[c, -e], [e, c]]))
        inv.append(np.stack(per))
    return (
        xt,
        np.stack(fwd).astype(ml_dtypes.bfloat16),
        np.stack(inv).astype(ml_dtypes.bfloat16),
    )


def cos_poly(z, terms):
    acc = jnp.full_like(z, (-1.0) ** terms / math.factorial(2 * terms))
    for k in range(terms - 1, -1, -1):
        acc = acc * z + (-1.0) ** k / math.factorial(2 * k)
    return acc


def sinc_poly(z, terms):
    acc = jnp.full_like(z, (-1.0) ** terms / math.factorial(2 * terms + 1))
    for k in range(terms - 1, -1, -1):
        acc = acc * z + (-1.0) ** k / math.factorial(2 * k + 1)
    return acc


def call(kernel, grid, in_specs, out_specs, out_shape, scratch=(), flops=0):
    return pl.pallas_call(
        kernel,
        out_shape=out_shape,
        grid_spec=pltpu.PrefetchScalarGridSpec(
            num_scalar_prefetch=2,
            grid=grid,
            in_specs=in_specs,
            out_specs=out_specs,
            scratch_shapes=list(scratch),
        ),
        compiler_params=pltpu.CompilerParams(vmem_limit_bytes=VMEM_LIMIT),
        cost_estimate=pl.CostEstimate(
            flops=flops, bytes_accessed=4 * 1024 * 1024, transcendentals=0
        ),
    )


def start_kernel(ints, reals, cell_ref, value_ref, out_ref, acc):
    core = ints[0]
    slab = 2 * pl.program_id(0) + core
    traces = cell_ref.shape[-1]
    chunk = 512
    acc[...] = jnp.zeros_like(acc)

    def add(i, carry):
        at = pl.ds(pl.multiple_of(i * chunk, chunk), chunk)
        cells = cell_ref[0, :, at]
        line = cells // NX
        col = cells - line * NX
        ylines = lax.broadcasted_iota(jnp.int32, (SLAB, chunk), 0)
        hit = ylines == line
        vals = value_ref[0, :, at].astype(f32)
        left = jnp.concatenate(
            [jnp.where(hit, vals[c : c + 1], 0.0).astype(bf16) for c in range(2)], axis=0
        )
        for j in range(NX // TILE):
            xcols = lax.broadcasted_iota(jnp.int32, (TILE, chunk), 0) + j * TILE
            right = jnp.where(xcols == col, 1.0, 0.0).astype(bf16)
            acc[:, j * TILE : (j + 1) * TILE] += lax.dot_general(
                left, right, (((1,), (1,)), ((), ())), preferred_element_type=f32
            )
        return carry

    lax.fori_loop(0, traces // chunk, add, 0)
    out_ref[1] = acc[...].astype(bf16).reshape(2, SLAB, NX)

    strip = 32

    def source(i, carry):
        at = pl.ds(pl.multiple_of(i * strip, strip), strip)
        line = lax.broadcasted_iota(jnp.int32, (strip, NX), 0) + (
            slab * SLAB + i * strip - ints[2]
        )
        col = lax.broadcasted_iota(jnp.int32, (strip, NX), 1) - ints[3]
        dy = line.astype(f32) * grid_step
        dx = col.astype(f32) * grid_step
        radius = jnp.sqrt(dy * dy + dx * dx + datum_depth**2)
        amplitude = datum_depth / radius
        phase = reals[0] * (radius * water_slowness)
        turns = jnp.floor(phase * (0.5 / math.pi) + 0.5)
        rest = phase - turns * 6.28125
        rest = rest - turns * (2.0 * math.pi - 6.28125)
        z = rest * rest
        cosine = amplitude * cos_poly(z, 9)
        sine = amplitude * (rest * sinc_poly(z, 9))
        out_ref[0, 0, at, :] = (reals[1] * cosine - reals[2] * sine).astype(bf16)
        out_ref[0, 1, at, :] = (reals[1] * sine + reals[2] * cosine).astype(bf16)
        return carry

    lax.fori_loop(0, SLAB // strip, source, 0)


def start_fields(ints, reals, cells, values):
    traces = cells.shape[-1]
    return call(
        start_kernel,
        (2,),
        [
            pl.BlockSpec((1, 1, traces), lambda i, a, b: (2 * i + a[0], 0, 0)),
            pl.BlockSpec((1, 2, traces), lambda i, a, b: (2 * i + a[0], 0, 0)),
        ],
        pl.BlockSpec((2, 2, SLAB, NX), lambda i, a, b: (0, 0, i, 0)),
        jax.ShapeDtypeStruct((2, 2, 2 * SLAB, NX), bf16),
        [pltpu.VMEM((2 * SLAB, NX), f32)],
        flops=8_000_000_000,
    )(ints, reals, cells, values)


def forward_x_kernel(ints, reals, wave_ref, table_ref, out_ref):
    rows = wave_ref.shape[2]
    left = wave_ref[...].reshape(4 * rows, NX)
    cos_part = jnp.dot(left, table_ref[0], preferred_element_type=f32)
    sin_part = jnp.dot(left, table_ref[1], preferred_element_type=f32)
    cos_part = cos_part.reshape(2, 2, rows, -1)
    sin_part = sin_part.reshape(2, 2, rows, -1)
    out_ref[:, 0] = (cos_part[:, 0] + sin_part[:, 1]).astype(bf16)
    out_ref[:, 1] = (cos_part[:, 1] - sin_part[:, 0]).astype(bf16)


def forward_x(ints, reals, wave, table, other):
    def half(a):
        return (1 - a[0]) if other else a[0]

    rows = wave.shape[2]
    tiles = HALF // TILE
    return call(
        forward_x_kernel,
        (tiles,),
        [
            pl.BlockSpec((2, 2, rows, NX), lambda i, a, b: (0, 0, 0, 0)),
            pl.BlockSpec((2, NX, TILE), lambda i, a, b: (0, 0, half(a) * tiles + i)),
        ],
        pl.BlockSpec((2, 2, rows, TILE), lambda i, a, b: (0, 0, 0, i)),
        jax.ShapeDtypeStruct((2, 2, rows, HALF), bf16),
        flops=4_000_000_000,
    )(ints, reals, wave, table)


def middle_kernel(
    step, ints, reals, mine_ref, got_ref, fm_ref, fg_ref, im_ref, ig_ref, keep_ref, send_ref
):
    width = mine_ref.shape[-1]
    omega, slow, aniso = reals[0], reals[3 + step], reals[3 + STEPS + step]
    q = lax.broadcasted_iota(jnp.int32, (NY, width), 0)
    k = lax.broadcasted_iota(jnp.int32, (NY, width), 1)
    k = k + ints[0] * HALF + pl.program_id(0) * width
    q = jnp.where(q < NY // 2, q, q - NY).astype(f32) * (2.0 * math.pi / (NY * grid_step))
    k = jnp.where(k < NX // 2, k, k - NX).astype(f32) * (2.0 * math.pi / (NX * grid_step))
    base = omega * slow
    vertical = base * base - (1.0 + 2.0 * aniso) * (q * q + k * k)
    going = jnp.maximum(vertical, 0.0)
    z = going * (depth_step * depth_step)
    damping = jnp.exp(jnp.sqrt(jnp.maximum(-vertical, 0.0)) * (-depth_step))
    cosine = damping * cos_poly(z, 8)
    sine = damping * (jnp.sqrt(going) * depth_step * sinc_poly(z, 8))
    slabs = im_ref.shape[0]
    for g in range(2):
        spec = jnp.dot(
            fm_ref[0], mine_ref[g].reshape(4 * SLAB, width), preferred_element_type=f32
        ) + jnp.dot(fg_ref[0], got_ref[g].reshape(4 * SLAB, width), preferred_element_type=f32)
        re, im = spec[:NY], spec[NY:]
        sgn = sine if g == 0 else -sine
        shifted = jnp.concatenate(
            [(re * cosine - im * sgn).astype(bf16), (im * cosine + re * sgn).astype(bf16)], axis=0
        )
        for hi in range(slabs):
            at = slice(hi * SLAB, (hi + 1) * SLAB)
            for table, out in ((ig_ref, send_ref), (im_ref, keep_ref)):
                back = jnp.dot(table[hi, 0], shifted, preferred_element_type=f32).astype(bf16)
                out[g, 0, at] = back[:SLAB]
                out[g, 1, at] = back[SLAB:]


def middle(step, ints, reals, mine, got, fwd, inv):
    last = step == STEPS - 1
    slabs = 1 if last else 2
    rows = slabs * SLAB

    def low(a):
        return a[1] if last else 0

    width = TILE
    return call(
        functools.partial(middle_kernel, step),
        (HALF // width,),
        [
            pl.BlockSpec((2, 2, 2 * SLAB, width), lambda i, a, b: (0, 0, 0, i)),
            pl.BlockSpec((2, 2, 2 * SLAB, width), lambda i, a, b: (0, 0, 0, i)),
            pl.BlockSpec((1, 2 * NY, NY), lambda i, a, b: (a[0], 0, 0)),
            pl.BlockSpec((1, 2 * NY, NY), lambda i, a, b: (1 - a[0], 0, 0)),
            pl.BlockSpec((slabs, 1, 2 * SLAB, 2 * NY), lambda i, a, b: (low(a), a[0], 0, 0)),
            pl.BlockSpec((slabs, 1, 2 * SLAB, 2 * NY), lambda i, a, b: (low(a), 1 - a[0], 0, 0)),
        ],
        [pl.BlockSpec((2, 2, rows, width), lambda i, a, b: (0, 0, 0, i))] * 2,
        [jax.ShapeDtypeStruct((2, 2, rows, HALF), bf16)] * 2,
        flops=4_000_000_000,
    )(ints, reals, mine, got, fwd, fwd, inv, inv)


def inverse_x_kernel(
    step, ints, reals, keep_ref, got_ref, tm_ref, tg_ref, model_ref, block_ref, wave_ref, image_ref
):
    rows = keep_ref.shape[2]
    mine = keep_ref[...].reshape(4 * rows, HALF)
    got = got_ref[...].reshape(4 * rows, HALF)
    omega, slow_ref = reals[0], reals[3 + step]
    cos_part = jnp.dot(mine, tm_ref[0], preferred_element_type=f32) + jnp.dot(
        got, tg_ref[0], preferred_element_type=f32
    )
    sin_part = jnp.dot(mine, tm_ref[1], preferred_element_type=f32) + jnp.dot(
        got, tg_ref[1], preferred_element_type=f32
    )
    cos_part = cos_part.reshape(2, 2, rows, TILE)
    sin_part = sin_part.reshape(2, 2, rows, TILE)
    space_re = cos_part[:, 0] - sin_part[:, 1]
    space_im = cos_part[:, 1] + sin_part[:, 0]
    matrix = block_ref[step]
    width = matrix.shape[0]
    slabs = rows // SLAB
    for j in range(TILE // width):
        at = slice(j * width, (j + 1) * width)
        model = model_ref[j].astype(f32)
        slow = model[:, 0, 0].reshape(rows, width)
        aniso = model[:, 0, 1].reshape(rows, width)
        phase = omega * (slow - slow_ref) * depth_step
        z = phase * phase
        cosine = cos_poly(z, 7)
        sine = phase * sinc_poly(z, 7)
        coefficient = omega * (slow * aniso) * depth_step
        nexts = []
        for g in range(2):
            sgn = sine if g == 0 else -sine
            re, im = space_re[g, :, at], space_im[g, :, at]
            split_re = (re * cosine - im * sgn).astype(bf16)
            split_im = (im * cosine + re * sgn).astype(bf16)
            both = jnp.concatenate([split_re, split_im], axis=0)
            correction = jnp.dot(both, matrix, preferred_element_type=f32)
            scaled = coefficient if g == 0 else -coefficient
            next_re = (split_re.astype(f32) - scaled * correction[rows:]).astype(bf16)
            next_im = (split_im.astype(f32) + scaled * correction[:rows]).astype(bf16)
            wave_ref[g, 0, :, at] = next_re
            wave_ref[g, 1, :, at] = next_im
            nexts.append((next_re.astype(f32), next_im.astype(f32)))
        image = nexts[0][0] * nexts[1][0] + nexts[0][1] * nexts[1][1]
        image_ref[:, at] = image.astype(bf16)


def inverse_x(step, ints, reals, keep, got, table, model, block):
    last = step == STEPS - 1
    rows = keep.shape[2]
    slabs = rows // SLAB
    width = block.shape[-1]

    def low(a):
        return a[1] if last else 0

    return call(
        functools.partial(inverse_x_kernel, step),
        (NX // TILE,),
        [
            pl.BlockSpec((2, 2, rows, HALF), lambda i, a, b: (0, 0, 0, 0)),
            pl.BlockSpec((2, 2, rows, HALF), lambda i, a, b: (0, 0, 0, 0)),
            pl.BlockSpec((2, HALF, TILE), lambda i, a, b: (0, a[0], i)),
            pl.BlockSpec((2, HALF, TILE), lambda i, a, b: (0, 1 - a[0], i)),
            pl.BlockSpec(
                (TILE // width, slabs, 1, 2, SLAB, width),
                lambda i, a, b: (i, low(a), a[0], 0, 0, 0),
            ),
            pl.BlockSpec((STEPS, width, width), lambda i, a, b: (0, 0, 0)),
        ],
        [
            pl.BlockSpec((2, 2, rows, TILE), lambda i, a, b: (0, 0, 0, i)),
            pl.BlockSpec((rows, TILE), lambda i, a, b: (0, i)),
        ],
        [
            jax.ShapeDtypeStruct((2, 2, rows, NX), bf16),
            jax.ShapeDtypeStruct((rows, NX), bf16),
        ],
        flops=5_000_000_000,
    )(ints, reals, keep, got, table, table, model, block)


def body(
    nfreq,
    nlat,
    record,
    receiver_cell,
    source_cell,
    wavelet,
    frequency_index,
    slowness,
    anisotropy,
    reference_slowness,
    reference_anisotropy,
    correction_block,
):
    fi = lax.axis_index("freq")
    zi = lax.axis_index("lat")
    core = fi % 2
    zh = zi // 2
    fc = zi % 2
    own = fi - core + fc
    pair = [(i, i ^ 1) for i in range(nfreq)]
    swap = [
        ((2 * j + h) * nlat + 2 * a + c, (2 * j + c) * nlat + 2 * a + h)
        for j in range(nfreq // 2)
        for h in range(2)
        for a in range(nlat // 2)
        for c in range(2)
    ]
    xt, fwd, inv = (jnp.asarray(t) for t in tables())

    head = jnp.concatenate(
        [frequency_index.astype(f32), wavelet.reshape(-1)]
    )
    head_other = lax.ppermute(head, "freq", pair)
    head = jnp.where(core == fc, head, head_other)
    angular = head[0] * (2.0 * math.pi * freq_step)

    both = ("freq", "lat")
    values = lax.all_gather(record.astype(bf16), both)
    cells = lax.all_gather(receiver_cell, "lat")
    nrec = values.shape[-1]
    values = values.reshape((nfreq, nlat) + values.shape[1:3] + (nrec,))
    values = lax.dynamic_index_in_dim(values, own, 2, keepdims=False)
    values = values.transpose(1, 2, 0, 3).reshape(nlat, 2, nfreq * nrec)

    models = []
    for s in range(STEPS):
        model = jnp.stack([slowness[s], anisotropy[s]]).astype(bf16)
        model = lax.all_gather(model, both)
        width = model.shape[-1]
        model = model.reshape(nfreq, 2, 2, 2, SLAB, width)
        if width != SLAB:
            model = model.transpose(1, 2, 3, 4, 0, 5).reshape(2, 2, 2, SLAB, NX // SLAB, SLAB)
            model = model.transpose(4, 0, 1, 2, 3, 5)
        models.append(model)

    source_line = source_cell[0] // NX
    ints = jnp.stack([core, zh, source_line, source_cell[0] - source_line * NX]).astype(jnp.int32)
    reals = jnp.concatenate(
        [angular[None], head[1:3], reference_slowness, reference_anisotropy]
    )
    wave = start_fields(ints, reals, cells, values)
    images = []
    for s in range(STEPS):
        send = forward_x(ints, reals, wave, xt, True)
        got = lax.ppermute(send, "freq", pair)
        mine = forward_x(ints, reals, wave, xt, False)
        keep, send = middle(s, ints, reals, mine, got, fwd, inv)
        got = lax.ppermute(send, "freq", pair)
        wave, image = inverse_x(s, ints, reals, keep, got, xt, models[s], correction_block)
        if s < STEPS - 1:
            image = lax.dynamic_slice_in_dim(image, zh * SLAB, SLAB, 0)
        image = lax.ppermute(image, both, swap)
        image = lax.all_to_all(image, "freq", split_axis=1, concat_axis=0, tiled=True)
        image = image.reshape(nfreq, SLAB, NX // nfreq).astype(f32)
        images.append(jnp.sum(image, axis=0))
    wave = lax.ppermute(wave, both, swap)
    return jnp.stack(images), wave[:, None]


def solution(mesh):
    return jax.shard_map(
        functools.partial(body, mesh.shape["freq"], mesh.shape["lat"]),
        mesh=mesh,
        in_specs=(
            P(None, None, "lat", "freq"),
            P("lat", None),
            P(),
            P("freq", None),
            P("freq"),
            P(None, "lat", "freq"),
            P(None, "lat", "freq"),
            P(),
            P(),
            P(),
        ),
        out_specs=(P(None, "lat", "freq"), P(None, "freq", None, "lat", None)),
        check_vma=False,
    )
```

time: 474 us -> 221 us (0.47); the launches traced: 465 us -> 219 us
  other arithmetic: 218 us -> 6.14 us
  Pallas kernels: 0 us -> 69.7 us
  local copies, waits for them, and re-layouts: 53.7 us -> 6.64 us
  waiting for transfers between devices: 59.9 us -> 16.5 us
  matrix products: 29.9 us -> 0 us
  blocking collectives: 68.1 us -> 88.5 us
    another operation x24 -> x6, other arithmetic: 126 us -> 3.85 us
    scatter-add x3 -> x0, other arithmetic: 74.1 us -> none  [body(): jnp.zeros((nfreqs * 2, slab_cells), jnp.float32).at[:, targets].add(values)]
    pallas_call x0 -> x9, Pallas kernels: none -> 69.7 us  [the longest x2 23.8 us: middle(): call(functools.partial(middle_kernel, step), (HALF // width,), [pl.BlockS...]
    all_gather x4 -> x2, blocking collectives: 36.8 us -> 88.5 us  [the longest x1 75.1 us: body(): values = lax.all_gather(record.astype(bf16), both)]
    reduce_scatter x2 -> x0, waiting for transfers between devices: 37.3 us -> none  [body(): lax.psum_scatter(imaging.astype(jnp.bfloat16), 'freq', scatter_dimension=...]
    all_to_all x1 -> x0, blocking collectives: 31.3 us -> none  [body(): lax.all_to_all(x_spectrum, 'lat', split_axis=4, concat_axis=3, tiled=True)]
    dot_general x10 -> x0, matrix products: 29.9 us -> none  [the longest x2 9.72 us: body(): jnp.einsum('gfcyx,cxdk->gfdyk', back_rows, inverse_x, preferred_element_t...]
    unnamed x56 -> x10, local copies, waits for them, and re-layouts: 28.2 us -> 4.93 us
  transfers between devices with their start and end apart: 6 -> 12, of which waited for: 4 -> 4; matrix products, arithmetic and copies ran while one was open for 27% -> 3% of each run, Pallas kernels for 0% -> 32%
where the time goes in v1:
time: 221 us; the launch traced here: 219 us
  blocking collectives  88.5 us (40%)
  Pallas kernels  69.7 us (32%)
  waiting for transfers between devices  16.5 us (7%)
  starting transfers between devices  16.3 us (7%)
  between operations  15.6 us (7%)
  local copies, waits for them, and re-layouts  6.64 us (3%)
  other arithmetic  6.14 us (3%)
    all_gather x1, blocking collectives, body(): values = lax.all_gather(record.astype(bf16), both)  75.1 us
    pallas_call x2, Pallas kernels, middle(): call(functools.partial(middle_kernel, step), (HALF // width,), [pl.BlockS...  23.8 us
    pallas_call x4, Pallas kernels, forward_x(): call(forward_x_kernel, (tiles,), [pl.BlockSpec((2, 2, rows, NX), lambda i...  17.7 us
    pallas_call x2, Pallas kernels, inverse_x(): call(functools.partial(inverse_x_kernel, step), (NX // TILE,), [pl.BlockS...  17 us
    all_gather x1, blocking collectives, body(): cells = lax.all_gather(receiver_cell, 'lat')  13.4 us
    all_to_all x2, waiting for transfers between devices, body(): lax.all_to_all(image, 'freq', split_axis=1, concat_axis=0, tiled=True)  13.1 us
    all_to_all x2, starting transfers between devices, body(): lax.all_to_all(image, 'freq', split_axis=1, concat_axis=0, tiled=True)  12.4 us
    pallas_call x1, Pallas kernels, start_fields(): call(start_kernel, (2,), [pl.BlockSpec((1, 1, traces), lambda i, a, b: (2...  11.2 us
  transfers between devices with their start and end apart: 12, of which 4 were waited for; matrix products, arithmetic and copies ran while one was open for 3% of the time, Pallas kernels for 32%

profile of v1, /device:TPU:0, one launch (start us, length us, event | category | flops | bytes accessed | tf_op | source)
XLA Modules:
  0.0 219.4 jit_solution(858236528802307836)
XLA Ops:
  7.2 0.9 convert.16
  8.1 0.9 convert.17
  10.4 0.7 pad_maximum_fusion.3
  11.6 0.8 copy.28
  12.4 75.1 %all-gather.1 = bf16[256,2,1,512]{3,1,2,0:T(2,128)(2,1)S(1)} all-gather(bf16[8,2,1,512]{3,1,2,0:T(2,128)(2,1)S(1)} %copy.28), channel_id=3, replica_groups=mesh['freq'=8,'lat'=4] {'freq','lat'}, dimensions={0}, use_global_device_ids=true | all-gather | bytes 540672 | tf_op jit(solution)/shard_map/all_gather | solution.py:375
  88.3 13.4 %all-gather.2.cell_ref = s32[4,1,4096]{2,1,0:T(1,128)S(1)} all-gather(s32[1,1,4096]{2,1,0:T(1,128)} %bitcast.51), channel_id=2, replica_groups=mesh['freq'=8,'lat'=4] {'lat'}, dimensions={0}, use_global_device_ids=true | all-gather | bytes 81920 | tf_op jit(solution)/shard_map/all_gather | solution.py:376
  101.8 0.7 broadcast_select_fusion
  102.6 0.8 pad_maximum_fusion.4.reals
  103.4 11.2 %shard_map.140.wave_ref = bf16[2,2,256,1024]{3,2,1,0:T(8,128)(2,1)S(1)} custom-call(s32[4]{0:T(128)S(1)} %pad_add_fusion.ints, f32[7]{0:T(128)S(1)} %pad_maximum_fusion.4.reals, s32[4,1,4096]{2,1,0:T(1,128)S(1)} %all-gather.2.cell_ref, bf16[4,2,4096]{2,1,0:T(2,128)(2,1)S(1)} %reshape.96.value_ref), custom_call_target="tpu_custom_call" | custom-call | flops 8000000000 | bytes 4194304 | tf_op jit(solution)/shard_map/pallas_call | solution.py:149
  114.6 4.6 %shard_map.142 = bf16[2,2,256,512]{3,2,1,0:T(8,128)(2,1)S(1)} custom-call(s32[4]{0:T(128)S(1)} %pad_add_fusion.ints, f32[7]{0:T(128)S(1)} %pad_maximum_fusion.4.reals, bf16[2,2,256,1024]{3,2,1,0:T(8,128)(2,1)S(1)} %shard_map.140.wave_ref, bf16[2,1024,1024]{2,1,0:T(8,128)(2,1)} %constant.70.clone.table_ref.tm_ref.tg_ref), custom_call_target="tpu_custom_call" | custom-call | flops 4000000000 | bytes 4194304 | tf_op jit(solution)/shard_map/pallas_call | solution.py:180
  119.9 1.6 copy-done.3
  121.5 4.4 %shard_map.141.mine_ref = bf16[2,2,256,512]{3,2,1,0:T(8,128)(2,1)S(1)} custom-call(s32[4]{0:T(128)S(1)} %pad_add_fusion.ints, f32[7]{0:T(128)S(1)} %pad_maximum_fusion.4.reals, bf16[2,2,256,1024]{3,2,1,0:T(8,128)(2,1)S(1)} %copy-done.3, bf16[2,1024,1024]{2,1,0:T(8,128)(2,1)} %constant.70.clone.table_ref.tm_ref.tg_ref), custom_call_target="tpu_custom_call" | custom-call | flops 4000000000 | bytes 4194304 | tf_op jit(solution)/shard_map/pallas_call | solution.py:180
  125.9 12.1 %shard_map.143 = (bf16[2,2,256,512]{3,2,1,0:T(8,128)(2,1)S(1)}, bf16[2,2,256,512]{3,2,1,0:T(8,128)(2,1)S(1)}) custom-call(s32[4]{0:T(128)S(1)} %pad_add_fusion.ints, f32[7]{0:T(128)S(1)} %pad_maximum_fusion.4.reals, bf16[2,2,256,512]{3,2,1,0:T(8,128)(2,1)S(1)} %shard_map.141.mine_ref, bf16[2,2,256,512]{3,2,1,0:T(8,128)(2,1)} %collective-permute-done.1.got_ref, ...), custom_call_target="tpu_custom_call" | custom-call | flops 4000000000 | bytes 4194304 | tf_op jit(solution)/shard_map/pallas_call | solution.py:237
  138.6 2.3 %collective-permute-done.2.got_ref = bf16[2,2,256,512]{3,2,1,0:T(8,128)(2,1)S(1)} collective-permute-done((bf16[2,2,256,512]{3,2,1,0:T(8,128)(2,1)S(1)}, bf16[2,2,256,512]{3,2,1,0:T(8,128)(2,1)S(1)}, u32[]{:S(2)}, u32[]{:S(2)}) %collective-permute-start.2) | collective-permute-done | bytes 1048608 | tf_op jit(solution)/shard_map/ppermute | solution.py:405
  140.9 10.7 %shard_map.144 = (bf16[2,2,256,1024]{3,2,1,0:T(8,128)(2,1)}, bf16[256,1024]{1,0:T(8,128)(2,1)S(1)}) custom-call(s32[4]{0:T(128)S(1)} %pad_add_fusion.ints, f32[7]{0:T(128)S(1)} %pad_maximum_fusion.4.reals, bf16[2,2,256,512]{3,2,1,0:T(8,128)(2,1)S(1)} %get-tuple-element.10.keep_ref, bf16[2,2,256,512]{3,2,1,0:T(8,128)(2,1)S(1)} %collective-permute-done.2.got_ref, ...), custom_call_target="tpu_custom_call" | custom-call | flops 5000000000 | bytes 4194304 | tf_op jit(solution)/shard_map/pallas_call | solution.py:311
  151.5 1.6 copy-done.1
  153.1 4.4 %shard_map.146 = bf16[2,2,256,512]{3,2,1,0:T(8,128)(2,1)S(1)} custom-call(s32[4]{0:T(128)S(1)} %pad_add_fusion.ints, f32[7]{0:T(128)S(1)} %pad_maximum_fusion.4.reals, bf16[2,2,256,1024]{3,2,1,0:T(8,128)(2,1)S(1)} %copy-done.1, bf16[2,1024,1024]{2,1,0:T(8,128)(2,1)} %constant.70.clone.table_ref.tm_ref.tg_ref), custom_call_target="tpu_custom_call" | custom-call | flops 4000000000 | bytes 4194304 | tf_op jit(solution)/shard_map/pallas_call | solution.py:180
  157.9 4.4 %shard_map.145.mine_ref = bf16[2,2,256,512]{3,2,1,0:T(8,128)(2,1)S(1)} custom-call(s32[4]{0:T(128)S(1)} %pad_add_fusion.ints, f32[7]{0:T(128)S(1)} %pad_maximum_fusion.4.reals, bf16[2,2,256,1024]{3,2,1,0:T(8,128)(2,1)S(1)} %copy-done.1, bf16[2,1024,1024]{2,1,0:T(8,128)(2,1)} %constant.70.clone.table_ref.tm_ref.tg_ref), custom_call_target="tpu_custom_call" | custom-call | flops 4000000000 | bytes 4194304 | tf_op jit(solution)/shard_map/pallas_call | solution.py:180
  162.3 11.7 %shard_map.147 = (bf16[2,2,128,512]{3,2,1,0:T(8,128)(2,1)S(1)}, bf16[2,2,128,512]{3,2,1,0:T(8,128)(2,1)S(1)}) custom-call(s32[4]{0:T(128)S(1)} %pad_add_fusion.ints, f32[7]{0:T(128)S(1)} %pad_maximum_fusion.4.reals, bf16[2,2,256,512]{3,2,1,0:T(8,128)(2,1)S(1)} %shard_map.145.mine_ref, bf16[2,2,256,512]{3,2,1,0:T(8,128)(2,1)S(1)} %collective-permute-done.4.got_ref, ...), custom_call_target="tpu_custom_call" | custom-call | flops 4000000000 | bytes 4194304 | tf_op jit(solution)/shard_map/pallas_call | solution.py:237
  174.3 0.7 collective-permute-start.3
  175.0 1.0 collective-permute-done.5.got_ref
  176.0 6.4 %shard_map.148 = (bf16[2,2,128,1024]{3,2,1,0:T(8,128)(2,1)S(1)}, bf16[128,1024]{1,0:T(8,128)(2,1)S(1)}) custom-call(s32[4]{0:T(128)S(1)} %pad_add_fusion.ints, f32[7]{0:T(128)S(1)} %pad_maximum_fusion.4.reals, bf16[2,2,128,512]{3,2,1,0:T(8,128)(2,1)S(1)} %get-tuple-element.14.keep_ref, bf16[2,2,128,512]{3,2,1,0:T(8,128)(2,1)S(1)} %collective-permute-done.5.got_ref, ...), custom_call_target="tpu_custom_call" | custom-call | flops 5000000000 | bytes 4194304 | tf_op jit(solution)/shard_map/pallas_call | solution.py:311
  182.4 0.7 collective-permute-start.7
  183.1 0.7 collective-permute-start.6
  183.8 0.7 copy_bitcast_fusion.1
  184.6 6.0 %all-to-all-start = ((bf16[128,8,128]{2,0,1:T(8,128)(2,1)}), bf16[128,8,128]{2,0,1:T(8,128)(2,1)S(1)}, u32[]{:S(2)}, u32[]{:S(2)}) async-start(bf16[128,8,128]{2,0,1:T(8,128)(2,1)} %copy_bitcast_fusion.1), calls=%async_computation | async-start | bytes 524288 | tf_op jit(solution)/shard_map/all_to_all | solution.py:410
  190.6 0.8 copy_bitcast_fusion
  191.4 6.2 %all-to-all-done = bf16[128,8,128]{2,0,1:T(8,128)(2,1)S(1)} async-done(((bf16[128,8,128]{2,0,1:T(8,128)(2,1)}), bf16[128,8,128]{2,0,1:T(8,128)(2,1)S(1)}, u32[]{:S(2)}, u32[]{:S(2)}) %all-to-all-start) | async-done | bytes 262176 | tf_op jit(solution)/shard_map/all_to_all | solution.py:410
  197.5 6.4 %all-to-all-start.1 = ((bf16[128,8,128]{2,0,1:T(8,128)(2,1)}), bf16[128,8,128]{2,0,1:T(8,128)(2,1)S(1)}, u32[]{:S(2)}, u32[]{:S(2)}) async-start(bf16[128,8,128]{2,0,1:T(8,128)(2,1)} %copy_bitcast_fusion), calls=%async_computation.1 | async-start | bytes 524288 | tf_op jit(solution)/shard_map/all_to_all | solution.py:410
  204.0 6.9 %all-to-all-done.1 = bf16[128,8,128]{2,0,1:T(8,128)(2,1)S(1)} async-done(((bf16[128,8,128]{2,0,1:T(8,128)(2,1)}), bf16[128,8,128]{2,0,1:T(8,128)(2,1)S(1)}, u32[]{:S(2)}, u32[]{:S(2)}) %all-to-all-start.1) | async-done | bytes 262176 | tf_op jit(solution)/shard_map/all_to_all | solution.py:410
  210.9 0.7 pad_maximum_fusion
  211.6 1.0 copy.33
  (34 shorter events, 3.5 us)
Async XLA Ops:
  7.2 133.7 %all-gather.6.cloned.1.call-start = ((), (), s32[]{:S(2)}) async-start(), calls=%async_computation.2 | async-start | bytes 2162688 | tf_op jit(solution)/shard_map/all_gather | solution.py:385
  9.7 165.2 %all-gather.8.cloned.1.call-start = ((), (), s32[]{:S(2)}) async-start(), calls=%async_computation.3 | async-start | bytes 2162688 | tf_op jit(solution)/shard_map/all_gather | solution.py:385
  11.2 90.6 %collective-permute-start = (f32[3]{0:T(128)S(1)}, f32[3]{0:T(128)S(1)}, u32[]{:S(2)}, u32[]{:S(2)}) collective-permute-start(f32[3]{0:T(128)S(1)} %pad_maximum_fusion.3), channel_id=1, source_target_pairs={{0,4},{4,0},{8,12},{12,8},{16,20},{20,16},{24,28},{28,24},{1,5},{5... | collective-permute-start | bytes 44 | tf_op jit(solution)/shard_map/ppermute | solution.py:370
  114.6 4.6 %copy-start.2 = (bf16[2,2,256,1024]{3,2,1,0:T(8,128)(2,1)}, bf16[2,2,256,1024]{3,2,1,0:T(8,128)(2,1)S(1)}, u32[]{:S(2)}) copy-start(bf16[2,2,256,1024]{3,2,1,0:T(8,128)(2,1)S(1)} %shard_map.140.wave_ref) | copy-start | bytes 6291460
  119.2 6.7 %collective-permute-start.1 = (bf16[2,2,256,512]{3,2,1,0:T(8,128)(2,1)S(1)}, bf16[2,2,256,512]{3,2,1,0:T(8,128)(2,1)}, u32[]{:S(2)}, u32[]{:S(2)}) collective-permute-start(bf16[2,2,256,512]{3,2,1,0:T(8,128)(2,1)S(1)} %shard_map.142), channel_id=1, source_target_pairs={{0,4},{4,0},{8,12},{12,8},{16,20},{20,16},{24,28},{28,24},{1,5},{5... | collective-permute-start | bytes 3145736 | tf_op jit(solution)/shard_map/ppermute | solution.py:402
  119.9 1.6 copy-start.3
  125.9 15.0 %copy-start = (bf16[2,128,128]{2,1,0:T(8,128)(2,1)S(1)}, bf16[2,128,128]{2,1,0:T(8,128)(2,1)}, u32[]{:S(2)}) copy-start(bf16[2,128,128]{2,1,0:T(8,128)(2,1)} %block_ref.3) | copy-start | bytes 196612
  138.0 2.8 %collective-permute-start.2 = (bf16[2,2,256,512]{3,2,1,0:T(8,128)(2,1)S(1)}, bf16[2,2,256,512]{3,2,1,0:T(8,128)(2,1)S(1)}, u32[]{:S(2)}, u32[]{:S(2)}) collective-permute-start(bf16[2,2,256,512]{3,2,1,0:T(8,128)(2,1)S(1)} %get-tuple-element.11), channel_id=1, source_target_pairs={{0,4},{4,0},{8,12},{12,8},{16,20},{20,16},{24,28},{28,24},{1,5},{5... | collective-permute-start | bytes 3145736 | tf_op jit(solution)/shard_map/ppermute | solution.py:405
  151.5 1.6 copy-start.1
  157.5 4.8 %collective-permute-start.4 = (bf16[2,2,256,512]{3,2,1,0:T(8,128)(2,1)S(1)}, bf16[2,2,256,512]{3,2,1,0:T(8,128)(2,1)S(1)}, u32[]{:S(2)}, u32[]{:S(2)}) collective-permute-start(bf16[2,2,256,512]{3,2,1,0:T(8,128)(2,1)S(1)} %shard_map.146), channel_id=1, source_target_pairs={{0,4},{4,0},{8,12},{12,8},{16,20},{20,16},{24,28},{28,24},{1,5},{5... | collective-permute-start | bytes 3145736 | tf_op jit(solution)/shard_map/ppermute | solution.py:402
  174.0 2.0 collective-permute-start.5
  174.3 9.6 %collective-permute-start.3 = (bf16[128,1024]{1,0:T(8,128)(2,1)S(1)}, bf16[128,1024]{1,0:T(8,128)(2,1)S(1)}, u32[]{:S(2)}, u32[]{:S(2)}) collective-permute-start(bf16[128,1024]{1,0:T(8,128)(2,1)S(1)} %constant_dynamic-slice_fusion), channel_id=1, source_target_pairs={{0,0},{1,4},{2,2},{3,6},{4,1},{5,5},{6,3},{7,7},{8,8},{9,12},{10,1... | collective-permute-start | bytes 786440 | tf_op jit(solution)/shard_map/ppermute | solution.py:409
  182.4 29.2 %collective-permute-start.7 = (bf16[2,2,128,1024]{3,2,1,0:T(8,128)(2,1)S(1)}, bf16[2,2,128,1024]{3,2,1,0:T(8,128)(2,1)S(1)}, u32[]{:S(2)}, u32[]{:S(2)}) collective-permute-start(bf16[2,2,128,1024]{3,2,1,0:T(8,128)(2,1)S(1)} %get-tuple-element.17), channel_id=1, source_target_pairs={{0,0},{1,4},{2,2},{3,6},{4,1},{5,5},{6,3},{7,7},{8,8},{9,12},{10,1... | collective-permute-start | bytes 3145736 | tf_op jit(solution)/shard_map/ppermute | solution.py:413
  183.1 7.5 %collective-permute-start.6 = (bf16[128,1024]{1,0:T(8,128)(2,1)S(1)}, bf16[128,1024]{1,0:T(8,128)(2,1)S(1)}, u32[]{:S(2)}, u32[]{:S(2)}) collective-permute-start(bf16[128,1024]{1,0:T(8,128)(2,1)S(1)} %get-tuple-element.16), channel_id=1, source_target_pairs={{0,0},{1,4},{2,2},{3,6},{4,1},{5,5},{6,3},{7,7},{8,8},{9,12},{10,1... | collective-permute-start | bytes 786440 | tf_op jit(solution)/shard_map/ppermute | solution.py:409
  184.6 13.0 %all-to-all-start = ((bf16[128,8,128]{2,0,1:T(8,128)(2,1)}), bf16[128,8,128]{2,0,1:T(8,128)(2,1)S(1)}, u32[]{:S(2)}, u32[]{:S(2)}) async-start(bf16[128,8,128]{2,0,1:T(8,128)(2,1)} %copy_bitcast_fusion.1), calls=%async_computation | async-start | bytes 524288 | tf_op jit(solution)/shard_map/all_to_all | solution.py:410
  197.5 13.3 %all-to-all-start.1 = ((bf16[128,8,128]{2,0,1:T(8,128)(2,1)}), bf16[128,8,128]{2,0,1:T(8,128)(2,1)S(1)}, u32[]{:S(2)}, u32[]{:S(2)}) async-start(bf16[128,8,128]{2,0,1:T(8,128)(2,1)} %copy_bitcast_fusion), calls=%async_computation.1 | async-start | bytes 524288 | tf_op jit(solution)/shard_map/all_to_all | solution.py:410
Sparse Core Ops, SparseCore 0:
  11.5 59.6 all-gather.5
  120.0 52.9 all-gather.7

commit v2 on v1

--- a/solution.py
+++ b/solution.py
@@ -24,7 +24,7 @@
 water_slowness = 1.0 / 1500.0
 f32 = jnp.float32
 bf16 = jnp.bfloat16
-VMEM_LIMIT = 50 * 1024 * 1024
+VMEM_LIMIT = 28 * 1024 * 1024
 
 
 def trig(length):
@@ -89,21 +89,21 @@
     )
 
 
-def start_kernel(ints, reals, cell_ref, value_ref, out_ref, acc):
+def start_kernel(ints, reals, packet_ref, out_ref, acc):
     core = ints[0]
     slab = 2 * pl.program_id(0) + core
-    traces = cell_ref.shape[-1]
+    traces = packet_ref.shape[-1]
     chunk = 512
     acc[...] = jnp.zeros_like(acc)
 
     def add(i, carry):
         at = pl.ds(pl.multiple_of(i * chunk, chunk), chunk)
-        cells = cell_ref[0, :, at]
+        cells = packet_ref[0, 2:3, at].astype(jnp.int32)
         line = cells // NX
         col = cells - line * NX
         ylines = lax.broadcasted_iota(jnp.int32, (SLAB, chunk), 0)
         hit = ylines == line
-        vals = value_ref[0, :, at].astype(f32)
+        vals = packet_ref[0, 0:2, at]
         left = jnp.concatenate(
             [jnp.where(hit, vals[c : c + 1], 0.0).astype(bf16) for c in range(2)], axis=0
         )
@@ -144,20 +144,17 @@
     lax.fori_loop(0, SLAB // strip, source, 0)
 
 
-def start_fields(ints, reals, cells, values):
-    traces = cells.shape[-1]
+def start_fields(ints, reals, packets):
+    traces = packets.shape[-1]
     return call(
         start_kernel,
         (2,),
-        [
-            pl.BlockSpec((1, 1, traces), lambda i, a, b: (2 * i + a[0], 0, 0)),
-            pl.BlockSpec((1, 2, traces), lambda i, a, b: (2 * i + a[0], 0, 0)),
-        ],
+        [pl.BlockSpec((1, 4, traces), lambda i, a, b: (i + a[1] - 2 * i * a[1], 0, 0))],
         pl.BlockSpec((2, 2, SLAB, NX), lambda i, a, b: (0, 0, i, 0)),
         jax.ShapeDtypeStruct((2, 2, 2 * SLAB, NX), bf16),
         [pltpu.VMEM((2 * SLAB, NX), f32)],
         flops=8_000_000_000,
-    )(ints, reals, cells, values)
+    )(ints, reals, packets)
 
 
 def forward_x_kernel(ints, reals, wave_ref, table_ref, out_ref):
@@ -252,8 +249,9 @@
 
 
 def inverse_x_kernel(
-    step, ints, reals, keep_ref, got_ref, tm_ref, tg_ref, model_ref, block_ref, wave_ref, image_ref
+    step, ints, reals, keep_ref, got_ref, tm_ref, tg_ref, *refs
 ):
+    *model_refs, block_ref, wave_ref, image_ref = refs
     rows = keep_ref.shape[2]
     mine = keep_ref[...].reshape(4 * rows, HALF)
     got = got_ref[...].reshape(4 * rows, HALF)
@@ -273,9 +271,15 @@
     slabs = rows // SLAB
     for j in range(TILE // width):
         at = slice(j * width, (j + 1) * width)
-        model = model_ref[j].astype(f32)
-        slow = model[:, 0, 0].reshape(rows, width)
-        aniso = model[:, 0, 1].reshape(rows, width)
+        near = model_refs[0][j].astype(f32)
+        if slabs == 1:
+            slow, aniso = near[0], near[1]
+        else:
+            far = model_refs[1][j].astype(f32)
+            first = jnp.where(ints[1] == 0, near, far)
+            second = jnp.where(ints[1] == 0, far, near)
+            slow = jnp.concatenate([first[0], second[0]], axis=0)
+            aniso = jnp.concatenate([first[1], second[1]], axis=0)
         phase = omega * (slow - slow_ref) * depth_step
         z = phase * phase
         cosine = cos_poly(z, 7)
@@ -300,13 +304,8 @@
 
 
 def inverse_x(step, ints, reals, keep, got, table, model, block):
-    last = step == STEPS - 1
     rows = keep.shape[2]
-    slabs = rows // SLAB
     width = block.shape[-1]
-
-    def low(a):
-        return a[1] if last else 0
 
     return call(
         functools.partial(inverse_x_kernel, step),
@@ -316,10 +315,10 @@
             pl.BlockSpec((2, 2, rows, HALF), lambda i, a, b: (0, 0, 0, 0)),
             pl.BlockSpec((2, HALF, TILE), lambda i, a, b: (0, a[0], i)),
             pl.BlockSpec((2, HALF, TILE), lambda i, a, b: (0, 1 - a[0], i)),
-            pl.BlockSpec(
-                (TILE // width, slabs, 1, 2, SLAB, width),
-                lambda i, a, b: (i, low(a), a[0], 0, 0, 0),
-            ),
+        ]
+        + [pl.BlockSpec((TILE // width, 2, SLAB, width), lambda i, a, b: (i, 0, 0, 0))]
+        * len(model)
+        + [
             pl.BlockSpec((STEPS, width, width), lambda i, a, b: (0, 0, 0)),
         ],
         [
@@ -331,7 +330,7 @@
             jax.ShapeDtypeStruct((rows, NX), bf16),
         ],
         flops=5_000_000_000,
-    )(ints, reals, keep, got, table, table, model, block)
+    )(ints, reals, keep, got, table, table, *model, block)
 
 
 def body(
@@ -352,8 +351,6 @@
     zi = lax.axis_index("lat")
     core = fi % 2
     zh = zi // 2
-    fc = zi % 2
-    own = fi - core + fc
     pair = [(i, i ^ 1) for i in range(nfreq)]
     swap = [
         ((2 * j + h) * nlat + 2 * a + c, (2 * j + c) * nlat + 2 * a + h)
@@ -362,32 +359,42 @@
         for a in range(nlat // 2)
         for c in range(2)
     ]
+    cross = [
+        ((2 * j + h) * nlat + 2 * a + c, (2 * j + c) * nlat + 2 * (1 - a) + h)
+        for j in range(nfreq // 2)
+        for h in range(2)
+        for a in range(nlat // 2)
+        for c in range(2)
+    ]
     xt, fwd, inv = (jnp.asarray(t) for t in tables())
 
-    head = jnp.concatenate(
-        [frequency_index.astype(f32), wavelet.reshape(-1)]
-    )
-    head_other = lax.ppermute(head, "freq", pair)
-    head = jnp.where(core == fc, head, head_other)
+    both = ("freq", "lat")
+    moved = lax.all_to_all(record.astype(bf16), "freq", split_axis=0, concat_axis=3, tiled=True)
+    traces = receiver_cell.shape[-1]
+    scalars = jnp.concatenate([frequency_index.astype(f32), wavelet.reshape(-1)])
+    packet = jnp.concatenate(
+        [
+            moved.reshape(2, traces).astype(f32),
+            receiver_cell.astype(f32),
+            jnp.pad(scalars, (0, traces - 3))[None],
+        ]
+    )
+    near = lax.ppermute(packet, both, swap)
+    far = lax.ppermute(packet, both, cross)
+    packets = jnp.stack([near, far])
+    head = near[3, :3]
     angular = head[0] * (2.0 * math.pi * freq_step)
-
-    both = ("freq", "lat")
-    values = lax.all_gather(record.astype(bf16), both)
-    cells = lax.all_gather(receiver_cell, "lat")
-    nrec = values.shape[-1]
-    values = values.reshape((nfreq, nlat) + values.shape[1:3] + (nrec,))
-    values = lax.dynamic_index_in_dim(values, own, 2, keepdims=False)
-    values = values.transpose(1, 2, 0, 3).reshape(nlat, 2, nfreq * nrec)
 
     models = []
     for s in range(STEPS):
         model = jnp.stack([slowness[s], anisotropy[s]]).astype(bf16)
-        model = lax.all_gather(model, both)
+        model = lax.all_gather(model, "freq")
         width = model.shape[-1]
-        model = model.reshape(nfreq, 2, 2, 2, SLAB, width)
         if width != SLAB:
-            model = model.transpose(1, 2, 3, 4, 0, 5).reshape(2, 2, 2, SLAB, NX // SLAB, SLAB)
-            model = model.transpose(4, 0, 1, 2, 3, 5)
+            model = model.transpose(1, 2, 0, 3).reshape(2, SLAB, NX // SLAB, SLAB)
+            model = model.transpose(2, 0, 1, 3)
+        model_near = lax.ppermute(model, both, swap)
+        model = [model_near] if s == STEPS - 1 else [model_near, lax.ppermute(model, both, cross)]
         models.append(model)
 
     source_line = source_cell[0] // NX
@@ -395,7 +402,7 @@
     reals = jnp.concatenate(
         [angular[None], head[1:3], reference_slowness, reference_anisotropy]
     )
-    wave = start_fields(ints, reals, cells, values)
+    wave = start_fields(ints, reals, packets)
     images = []
     for s in range(STEPS):
         send = forward_x(ints, reals, wave, xt, True)
@@ -406,12 +413,13 @@
         wave, image = inverse_x(s, ints, reals, keep, got, xt, models[s], correction_block)
         if s < STEPS - 1:
             image = lax.dynamic_slice_in_dim(image, zh * SLAB, SLAB, 0)
-        image = lax.ppermute(image, both, swap)
-        image = lax.all_to_all(image, "freq", split_axis=1, concat_axis=0, tiled=True)
-        image = image.reshape(nfreq, SLAB, NX // nfreq).astype(f32)
-        images.append(jnp.sum(image, axis=0))
+        images.append(image)
+    images = lax.ppermute(jnp.stack(images), both, swap)
+    images = lax.all_to_all(
+        images.reshape(STEPS, SLAB, nfreq, NX // nfreq).transpose(2, 0, 1, 3), "freq", 0, 0, tiled=True
+    )
     wave = lax.ppermute(wave, both, swap)
-    return jnp.stack(images), wave[:, None]
+    return jnp.sum(images.astype(f32), axis=0), wave[:, None]
 
 
 def solution(mesh):

time: 221 us -> 160 us (0.72)
  blocking collectives: 88.5 us -> 39.9 us
  waiting for transfers between devices: 16.5 us -> 30 us
  between operations: 15.6 us -> 2.97 us
  Pallas kernels: 69.7 us -> 59.6 us
    all_gather x2, blocking collectives: 88.5 us -> 18.6 us  [body(): model = lax.all_gather(model, 'freq')]
    ppermute x3 -> x6, waiting for transfers between devices: 0.01 us -> 26.6 us  [the longest x1 24.7 us: body(): lax.ppermute(model, both, cross)]
    all_to_all x0 -> x1, blocking collectives: none -> 21.3 us  [body(): lax.all_to_all(images.reshape(STEPS, SLAB, nfreq, NX // nfreq).transpose(...]
    all_to_all x2 -> x1, waiting for transfers between devices: 13.1 us -> 1.93 us  [body(): lax.all_to_all(record.astype(bf16), 'freq', split_axis=0, concat_axis=3,...]
    all_to_all x2 -> x1, starting transfers between devices: 12.4 us -> 5.17 us  [body(): lax.all_to_all(record.astype(bf16), 'freq', split_axis=0, concat_axis=3,...]
    ppermute x3 -> x6, starting transfers between devices: 1.81 us -> 7.12 us  [the longest x1 2.65 us: body(): far = lax.ppermute(packet, both, cross)]
    pallas_call x2, Pallas kernels: 23.8 us -> 19.7 us  [middle(): call(functools.partial(middle_kernel, step), (HALF // width,), [pl.BlockS...]
    pallas_call x4, Pallas kernels: 17.7 us -> 13.8 us  [forward_x(): call(forward_x_kernel, (tiles,), [pl.BlockSpec((2, 2, rows, NX), lambda i...]
  transfers between devices with their start and end apart: 12 -> 12, of which waited for: 4 -> 4; matrix products, arithmetic and copies ran while one was open for 3% -> 2% of each run, Pallas kernels for 32% -> 10%
where the time goes in v2:
time: 160 us; the launch traced here: 159 us
  Pallas kernels  59.6 us (37%)
  blocking collectives  39.9 us (25%)
  waiting for transfers between devices  30 us (19%)
  starting transfers between devices  18 us (11%)
  local copies, waits for them, and re-layouts  4.6 us (3%)
  other arithmetic  3.99 us (2%)
  between operations  2.97 us (2%)
    ppermute x1, waiting for transfers between devices, body(): lax.ppermute(model, both, cross)  24.7 us
    all_to_all x1, blocking collectives, body(): lax.all_to_all(images.reshape(STEPS, SLAB, nfreq, NX // nfreq).transpose(...  21.3 us
    pallas_call x2, Pallas kernels, middle(): call(functools.partial(middle_kernel, step), (HALF // width,), [pl.BlockS...  19.7 us
    all_gather x2, blocking collectives, body(): model = lax.all_gather(model, 'freq')  18.6 us
    pallas_call x2, Pallas kernels, inverse_x(): call(functools.partial(inverse_x_kernel, step), (NX // TILE,), [pl.BlockS...  14.9 us
    pallas_call x4, Pallas kernels, forward_x(): call(forward_x_kernel, (tiles,), [pl.BlockSpec((2, 2, rows, NX), lambda i...  13.8 us
    pallas_call x1, Pallas kernels, start_fields(): call(start_kernel, (2,), [pl.BlockSpec((1, 4, traces), lambda i, a, b: (i...  11.2 us
    all_to_all x1, starting transfers between devices, body(): lax.all_to_all(record.astype(bf16), 'freq', split_axis=0, concat_axis=3,...  5.17 us
  transfers between devices with their start and end apart: 12, of which 4 were waited for; matrix products, arithmetic and copies ran while one was open for 2% of the time, Pallas kernels for 10%

profile of v2, /device:TPU:0, one launch (start us, length us, event | category | flops | bytes accessed | tf_op | source)
XLA Modules:
  0.0 159.2 jit_solution(3421090791393709742)
XLA Ops:
  0.6 0.8 convert_element_type.42
  2.0 5.2 %all-to-all-start = ((bf16[8,2,512]{2,1,0:T(2,128)(2,1)}), bf16[8,2,512]{2,1,0:T(2,128)(2,1)S(1)}, u32[]{:S(2)}, u32[]{:S(2)}) async-start(bf16[8,2,512]{2,1,0:T(2,128)(2,1)} %bitcast.44), calls=%async_computation | async-start | bytes 32768 | tf_op jit(solution)/shard_map/all_to_all | solution.py:372
  7.9 0.7 select_maximum_fusion
  9.3 0.7 convert_element_type.47
  10.0 1.9 %all-to-all-done = bf16[8,2,512]{2,1,0:T(2,128)(2,1)S(1)} async-done(((bf16[8,2,512]{2,1,0:T(2,128)(2,1)}), bf16[8,2,512]{2,1,0:T(2,128)(2,1)S(1)}, u32[]{:S(2)}, u32[]{:S(2)}) %all-to-all-start) | async-done | bytes 16416 | tf_op jit(solution)/shard_map/all_to_all | solution.py:372
  12.8 2.7 %collective-permute-start.1 = (f32[4,4096]{1,0:T(4,128)S(1)}, f32[4,4096]{1,0:T(4,128)S(1)}, u32[]{:S(2)}, u32[]{:S(2)}) collective-permute-start(f32[4,4096]{1,0:T(4,128)S(1)} %pad_maximum_fusion.2), channel_id=1, source_target_pairs={{0,2},{1,6},{2,0},{3,4},{4,3},{5,7},{6,1},{7,5},{8,10},{9,14},{10,... | collective-permute-start | bytes 196616 | tf_op jit(solution)/shard_map/ppermute | solution.py:383
  16.7 1.9 %collective-permute-done.1 = f32[4,4096]{1,0:T(4,128)S(1)} collective-permute-done((f32[4,4096]{1,0:T(4,128)S(1)}, f32[4,4096]{1,0:T(4,128)S(1)}, u32[]{:S(2)}, u32[]{:S(2)}) %collective-permute-start.1) | collective-permute-done | bytes 65568 | tf_op jit(solution)/shard_map/ppermute | solution.py:383
  18.6 0.7 pad_maximum_fusion.5.reals
  19.4 11.2 %shard_map.140.wave_ref = bf16[2,2,256,1024]{3,2,1,0:T(8,128)(2,1)S(1)} custom-call(s32[4]{0:T(128)S(1)} %pad_add_fusion.ints, f32[7]{0:T(128)S(1)} %pad_maximum_fusion.5.reals, f32[2,4,4096]{2,1,0:T(4,128)S(1)} %pad_maximum_fusion.1.packet_ref), custom_call_target="tpu_custom_call" | custom-call | flops 8000000000 | bytes 4194304 | tf_op jit(solution)/shard_map/pallas_call | solution.py:149
  30.6 3.5 %shard_map.142 = bf16[2,2,256,512]{3,2,1,0:T(8,128)(2,1)S(1)} custom-call(s32[4]{0:T(128)S(1)} %pad_add_fusion.ints, f32[7]{0:T(128)S(1)} %pad_maximum_fusion.5.reals, bf16[2,2,256,1024]{3,2,1,0:T(8,128)(2,1)S(1)} %shard_map.140.wave_ref, bf16[2,1024,1024]{2,1,0:T(8,128)(2,1)S(1)} %copy-done.1), custom_call_target="tpu_custom_call" | custom-call | flops 4000000000 | bytes 4194304 | tf_op jit(solution)/shard_map/pallas_call | solution.py:177
  34.1 2.8 %collective-permute-start.2 = (bf16[2,2,256,512]{3,2,1,0:T(8,128)(2,1)S(1)}, bf16[2,2,256,512]{3,2,1,0:T(8,128)(2,1)S(1)}, u32[]{:S(2)}, u32[]{:S(2)}) collective-permute-start(bf16[2,2,256,512]{3,2,1,0:T(8,128)(2,1)S(1)} %shard_map.142), channel_id=1, source_target_pairs={{0,4},{4,0},{8,12},{12,8},{16,20},{20,16},{24,28},{28,24},{1,5},{5... | collective-permute-start | bytes 3145736 | tf_op jit(solution)/shard_map/ppermute | solution.py:409
  36.9 3.5 %shard_map.141.mine_ref = bf16[2,2,256,512]{3,2,1,0:T(8,128)(2,1)S(1)} custom-call(s32[4]{0:T(128)S(1)} %pad_add_fusion.ints, f32[7]{0:T(128)S(1)} %pad_maximum_fusion.5.reals, bf16[2,2,256,1024]{3,2,1,0:T(8,128)(2,1)S(1)} %shard_map.140.wave_ref, bf16[2,1024,1024]{2,1,0:T(8,128)(2,1)S(1)} %copy-done.1), custom_call_target="tpu_custom_call" | custom-call | flops 4000000000 | bytes 4194304 | tf_op jit(solution)/shard_map/pallas_call | solution.py:177
  40.4 10.0 %shard_map.143 = (bf16[2,2,256,512]{3,2,1,0:T(8,128)(2,1)S(1)}, bf16[2,2,256,512]{3,2,1,0:T(8,128)(2,1)S(1)}) custom-call(s32[4]{0:T(128)S(1)} %pad_add_fusion.ints, f32[7]{0:T(128)S(1)} %pad_maximum_fusion.5.reals, bf16[2,2,256,512]{3,2,1,0:T(8,128)(2,1)S(1)} %shard_map.141.mine_ref, bf16[2,2,256,512]{3,2,1,0:T(8,128)(2,1)S(1)} %collective-permute-done.2.got_ref, ...), custom_call_target="tpu_custom_call" | custom-call | flops 4000000000 | bytes 4194304 | tf_op jit(solution)/shard_map/pallas_call | solution.py:234
  50.6 8.9 %all_gather.8 = bf16[8,2,128,128]{3,2,1,0:T(8,128)(2,1)S(1)} all-gather(bf16[1,2,128,128]{3,2,1,0:T(8,128)(2,1)S(1)} %pad_maximum_fusion.3), channel_id=1, replica_groups=mesh['freq'=8,'lat'=4] {'freq'}, dimensions={0}, use_global_device_ids=true | all-gather | bytes 589824 | tf_op jit(solution)/shard_map/all_gather | solution.py:391
  59.5 0.7 collective-permute-start.4
  60.2 1.6 collective-permute-start.5
  61.8 24.7 %collective-permute-done.5.refs_1_ = bf16[8,2,128,128]{3,2,1,0:T(8,128)(2,1)S(1)} collective-permute-done((bf16[8,2,128,128]{3,2,1,0:T(8,128)(2,1)S(1)}, bf16[8,2,128,128]{3,2,1,0:T(8,128)(2,1)S(1)}, u32[]{:S(2)}, u32[]{:S(2)}) %collective-permute-start.5) | collective-permute-done | bytes 524320 | tf_op jit(solution)/shard_map/ppermute | solution.py:397
  86.5 9.4 %shard_map.144 = (bf16[2,2,256,1024]{3,2,1,0:T(8,128)(2,1)S(1)}, bf16[256,1024]{1,0:T(8,128)(2,1)S(1)}) custom-call(s32[4]{0:T(128)S(1)} %pad_add_fusion.ints, f32[7]{0:T(128)S(1)} %pad_maximum_fusion.5.reals, bf16[2,2,256,512]{3,2,1,0:T(8,128)(2,1)S(1)} %get-tuple-element.10.keep_ref, bf16[2,2,256,512]{3,2,1,0:T(8,128)(2,1)S(1)} %collective-permute-done.3.got_ref, ...), custom_call_target="tpu_custom_call" | custom-call | flops 5000000000 | bytes 4194304 | tf_op jit(solution)/shard_map/pallas_call | solution.py:310
  95.9 3.5 %shard_map.146 = bf16[2,2,256,512]{3,2,1,0:T(8,128)(2,1)S(1)} custom-call(s32[4]{0:T(128)S(1)} %pad_add_fusion.ints, f32[7]{0:T(128)S(1)} %pad_maximum_fusion.5.reals, bf16[2,2,256,1024]{3,2,1,0:T(8,128)(2,1)S(1)} %get-tuple-element.13.wave_ref, bf16[2,1024,1024]{2,1,0:T(8,128)(2,1)S(1)} %copy-done.1), custom_call_target="tpu_custom_call" | custom-call | flops 4000000000 | bytes 4194304 | tf_op jit(solution)/shard_map/pallas_call | solution.py:177
  99.5 9.7 %all_gather.9 = bf16[8,2,128,128]{3,2,1,0:T(8,128)(2,1)S(1)} all-gather(bf16[1,2,128,128]{3,2,1,0:T(8,128)(2,1)S(1)} %pad_maximum_fusion.4), channel_id=1, replica_groups=mesh['freq'=8,'lat'=4] {'freq'}, dimensions={0}, use_global_device_ids=true | all-gather | bytes 589824 | tf_op jit(solution)/shard_map/all_gather | solution.py:391
  109.2 0.9 collective-permute-start.8
  110.0 3.4 %shard_map.145.mine_ref = bf16[2,2,256,512]{3,2,1,0:T(8,128)(2,1)S(1)} custom-call(s32[4]{0:T(128)S(1)} %pad_add_fusion.ints, f32[7]{0:T(128)S(1)} %pad_maximum_fusion.5.reals, bf16[2,2,256,1024]{3,2,1,0:T(8,128)(2,1)S(1)} %get-tuple-element.13.wave_ref, bf16[2,1024,1024]{2,1,0:T(8,128)(2,1)S(1)} %copy-done.1), custom_call_target="tpu_custom_call" | custom-call | flops 4000000000 | bytes 4194304 | tf_op jit(solution)/shard_map/pallas_call | solution.py:177
  113.5 9.7 %shard_map.147 = (bf16[2,2,128,512]{3,2,1,0:T(8,128)(2,1)S(1)}, bf16[2,2,128,512]{3,2,1,0:T(8,128)(2,1)S(1)}) custom-call(s32[4]{0:T(128)S(1)} %pad_add_fusion.ints, f32[7]{0:T(128)S(1)} %pad_maximum_fusion.5.reals, bf16[2,2,256,512]{3,2,1,0:T(8,128)(2,1)S(1)} %shard_map.145.mine_ref, bf16[2,2,256,512]{3,2,1,0:T(8,128)(2,1)S(1)} %collective-permute-done.6.got_ref, ...), custom_call_target="tpu_custom_call" | custom-call | flops 4000000000 | bytes 4194304 | tf_op jit(solution)/shard_map/pallas_call | solution.py:234
  123.2 2.1 %collective-permute-start.7 = (bf16[2,2,128,512]{3,2,1,0:T(8,128)(2,1)S(1)}, bf16[2,2,128,512]{3,2,1,0:T(8,128)(2,1)S(1)}, u32[]{:S(2)}, u32[]{:S(2)}) collective-permute-start(bf16[2,2,128,512]{3,2,1,0:T(8,128)(2,1)S(1)} %get-tuple-element.15), channel_id=1, source_target_pairs={{0,4},{4,0},{8,12},{12,8},{16,20},{20,16},{24,28},{28,24},{1,5},{5... | collective-permute-start | bytes 1572872 | tf_op jit(solution)/shard_map/ppermute | solution.py:412
  125.3 1.5 collective-permute-done.7.got_ref
  126.8 2.2 %copy-done.2 = bf16[2,1024,1024]{2,1,0:T(8,128)(2,1)S(1)} copy-done((bf16[2,1024,1024]{2,1,0:T(8,128)(2,1)S(1)}, bf16[2,1024,1024]{2,1,0:T(8,128)(2,1)}, u32[]{:S(2)}) %copy-start.2) | copy-done | bytes 4194328
  129.0 5.5 %shard_map.148 = (bf16[2,2,128,1024]{3,2,1,0:T(8,128)(2,1)S(1)}, bf16[128,1024]{1,0:T(8,128)(2,1)S(1)}) custom-call(s32[4]{0:T(128)S(1)} %pad_add_fusion.ints, f32[7]{0:T(128)S(1)} %pad_maximum_fusion.5.reals, bf16[2,2,128,512]{3,2,1,0:T(8,128)(2,1)S(1)} %get-tuple-element.14.keep_ref, bf16[2,2,128,512]{3,2,1,0:T(8,128)(2,1)S(1)} %collective-permute-done.7.got_ref, ...), custom_call_target="tpu_custom_call" | custom-call | flops 5000000000 | bytes 4194304 | tf_op jit(solution)/shard_map/pallas_call | solution.py:310
  134.6 0.7 collective-permute-start.9
  135.3 0.7 collective-permute-start.10
  136.2 21.3 %all_to_all.14 = bf16[8,2,128,128]{3,2,1,0:T(8,128)(2,1)S(1)} all-to-all(bf16[8,2,128,128]{3,2,1,0:T(8,128)(2,1)S(1)} %bitcast_bitcast_fusion), channel_id=1, replica_groups=mesh['freq'=8,'lat'=4] {'freq'}, dimensions={0} | all-to-all | bytes 1048576 | tf_op jit(solution)/shard_map/all_to_all | solution.py:418
  157.5 0.7 convert_reduce_fusion
  158.2 1.0 copy.29
  (41 shorter events, 2.6 us)
Async XLA Ops:
  2.0 9.9 %all-to-all-start = ((bf16[8,2,512]{2,1,0:T(2,128)(2,1)}), bf16[8,2,512]{2,1,0:T(2,128)(2,1)S(1)}, u32[]{:S(2)}, u32[]{:S(2)}) async-start(bf16[8,2,512]{2,1,0:T(2,128)(2,1)} %bitcast.44), calls=%async_computation | async-start | bytes 32768 | tf_op jit(solution)/shard_map/all_to_all | solution.py:372
  12.1 3.4 %collective-permute-start = (f32[4,4096]{1,0:T(4,128)S(1)}, f32[4,4096]{1,0:T(4,128)S(1)}, u32[]{:S(2)}, u32[]{:S(2)}) collective-permute-start(f32[4,4096]{1,0:T(4,128)S(1)} %pad_maximum_fusion.2), channel_id=1, source_target_pairs={{0,0},{1,4},{2,2},{3,6},{4,1},{5,5},{6,3},{7,7},{8,8},{9,12},{10,1... | collective-permute-start | bytes 196616 | tf_op jit(solution)/shard_map/ppermute | solution.py:382
  12.8 5.8 %collective-permute-start.1 = (f32[4,4096]{1,0:T(4,128)S(1)}, f32[4,4096]{1,0:T(4,128)S(1)}, u32[]{:S(2)}, u32[]{:S(2)}) collective-permute-start(f32[4,4096]{1,0:T(4,128)S(1)} %pad_maximum_fusion.2), channel_id=1, source_target_pairs={{0,2},{1,6},{2,0},{3,4},{4,3},{5,7},{6,1},{7,5},{8,10},{9,14},{10,... | collective-permute-start | bytes 196616 | tf_op jit(solution)/shard_map/ppermute | solution.py:383
  19.4 11.2 %copy-start.1 = (bf16[2,1024,1024]{2,1,0:T(8,128)(2,1)S(1)}, bf16[2,1024,1024]{2,1,0:T(8,128)(2,1)}, u32[]{:S(2)}) copy-start(bf16[2,1024,1024]{2,1,0:T(8,128)(2,1)} %constant.62.clone.table_ref.tm_ref.tg_ref) | copy-start | bytes 12582916
  34.1 6.3 %copy-start.3 = (bf16[2,1024,512]{2,1,0:T(8,128)(2,1)S(1)}, bf16[2,1024,512]{2,1,0:T(8,128)(2,1)}, u32[]{:S(2)}) copy-start(bf16[2,1024,512]{2,1,0:T(8,128)(2,1)} %constant.63.clone.fm_ref.fg_ref) | copy-start | bytes 6291460
  34.1 6.3 %copy-start.4 = (bf16[2,2,256,1024]{3,2,1,0:T(8,128)(2,1)S(1)}, bf16[2,2,256,1024]{3,2,1,0:T(8,128)(2,1)}, u32[]{:S(2)}) copy-start(bf16[2,2,256,1024]{3,2,1,0:T(8,128)(2,1)} %constant.64.clone.im_ref.ig_ref) | copy-start | bytes 6291460
  34.1 6.3 %collective-permute-start.2 = (bf16[2,2,256,512]{3,2,1,0:T(8,128)(2,1)S(1)}, bf16[2,2,256,512]{3,2,1,0:T(8,128)(2,1)S(1)}, u32[]{:S(2)}, u32[]{:S(2)}) collective-permute-start(bf16[2,2,256,512]{3,2,1,0:T(8,128)(2,1)S(1)} %shard_map.142), channel_id=1, source_target_pairs={{0,4},{4,0},{8,12},{12,8},{16,20},{20,16},{24,28},{28,24},{1,5},{5... | collective-permute-start | bytes 3145736 | tf_op jit(solution)/shard_map/ppermute | solution.py:409
  40.4 10.1 %copy-start.5 = (f32[2,128,128]{2,1,0:T(8,128)S(1)}, f32[2,128,128]{2,1,0:T(8,128)}, u32[]{:S(2)}) copy-start(f32[2,128,128]{2,1,0:T(8,128)} %param.18) | copy-start | bytes 393220
  40.4 10.1 %copy-start.6 = (f32[2,128,128]{2,1,0:T(8,128)S(1)}, f32[2,128,128]{2,1,0:T(8,128)}, u32[]{:S(2)}) copy-start(f32[2,128,128]{2,1,0:T(8,128)} %param.19) | copy-start | bytes 393220
  40.4 46.1 %copy-start = (bf16[2,128,128]{2,1,0:T(8,128)(2,1)S(1)}, bf16[2,128,128]{2,1,0:T(8,128)(2,1)}, u32[]{:S(2)}) copy-start(bf16[2,128,128]{2,1,0:T(8,128)(2,1)} %refs_1_.1) | copy-start | bytes 196612
  50.4 36.1 %collective-permute-start.3 = (bf16[2,2,256,512]{3,2,1,0:T(8,128)(2,1)S(1)}, bf16[2,2,256,512]{3,2,1,0:T(8,128)(2,1)S(1)}, u32[]{:S(2)}, u32[]{:S(2)}) collective-permute-start(bf16[2,2,256,512]{3,2,1,0:T(8,128)(2,1)S(1)} %get-tuple-element.11), channel_id=1, source_target_pairs={{0,4},{4,0},{8,12},{12,8},{16,20},{20,16},{24,28},{28,24},{1,5},{5... | collective-permute-start | bytes 3145736 | tf_op jit(solution)/shard_map/ppermute | solution.py:412
  59.5 2.3 %collective-permute-start.4 = (bf16[8,2,128,128]{3,2,1,0:T(8,128)(2,1)S(1)}, bf16[8,2,128,128]{3,2,1,0:T(8,128)(2,1)S(1)}, u32[]{:S(2)}, u32[]{:S(2)}) collective-permute-start(bf16[8,2,128,128]{3,2,1,0:T(8,128)(2,1)S(1)} %all_gather.8), channel_id=1, source_target_pairs={{0,0},{1,4},{2,2},{3,6},{4,1},{5,5},{6,3},{7,7},{8,8},{9,12},{10,1... | collective-permute-start | bytes 1572872 | tf_op jit(solution)/shard_map/ppermute | solution.py:396
  60.2 26.3 %collective-permute-start.5 = (bf16[8,2,128,128]{3,2,1,0:T(8,128)(2,1)S(1)}, bf16[8,2,128,128]{3,2,1,0:T(8,128)(2,1)S(1)}, u32[]{:S(2)}, u32[]{:S(2)}) collective-permute-start(bf16[8,2,128,128]{3,2,1,0:T(8,128)(2,1)S(1)} %all_gather.8), channel_id=1, source_target_pairs={{0,2},{1,6},{2,0},{3,4},{4,3},{5,7},{6,1},{7,5},{8,10},{9,14},{10,... | collective-permute-start | bytes 1572872 | tf_op jit(solution)/shard_map/ppermute | solution.py:397
  99.4 14.1 %collective-permute-start.6 = (bf16[2,2,256,512]{3,2,1,0:T(8,128)(2,1)S(1)}, bf16[2,2,256,512]{3,2,1,0:T(8,128)(2,1)S(1)}, u32[]{:S(2)}, u32[]{:S(2)}) collective-permute-start(bf16[2,2,256,512]{3,2,1,0:T(8,128)(2,1)S(1)} %shard_map.146), channel_id=1, source_target_pairs={{0,4},{4,0},{8,12},{12,8},{16,20},{20,16},{24,28},{28,24},{1,5},{5... | collective-permute-start | bytes 3145736 | tf_op jit(solution)/shard_map/ppermute | solution.py:409
  109.2 16.2 %collective-permute-start.8 = (bf16[8,2,128,128]{3,2,1,0:T(8,128)(2,1)S(1)}, bf16[8,2,128,128]{3,2,1,0:T(8,128)(2,1)S(1)}, u32[]{:S(2)}, u32[]{:S(2)}) collective-permute-start(bf16[8,2,128,128]{3,2,1,0:T(8,128)(2,1)S(1)} %all_gather.9), channel_id=1, source_target_pairs={{0,0},{1,4},{2,2},{3,6},{4,1},{5,5},{6,3},{7,7},{8,8},{9,12},{10,1... | collective-permute-start | bytes 1572872 | tf_op jit(solution)/shard_map/ppermute | solution.py:396
  123.2 3.6 %collective-permute-start.7 = (bf16[2,2,128,512]{3,2,1,0:T(8,128)(2,1)S(1)}, bf16[2,2,128,512]{3,2,1,0:T(8,128)(2,1)S(1)}, u32[]{:S(2)}, u32[]{:S(2)}) collective-permute-start(bf16[2,2,128,512]{3,2,1,0:T(8,128)(2,1)S(1)} %get-tuple-element.15), channel_id=1, source_target_pairs={{0,4},{4,0},{8,12},{12,8},{16,20},{20,16},{24,28},{28,24},{1,5},{5... | collective-permute-start | bytes 1572872 | tf_op jit(solution)/shard_map/ppermute | solution.py:412
  126.8 2.2 %copy-start.2 = (bf16[2,1024,1024]{2,1,0:T(8,128)(2,1)S(1)}, bf16[2,1024,1024]{2,1,0:T(8,128)(2,1)}, u32[]{:S(2)}) copy-start(bf16[2,1024,1024]{2,1,0:T(8,128)(2,1)} %constant.62.clone.table_ref.tm_ref.tg_ref) | copy-start | bytes 12582916
  134.6 1.4 collective-permute-start.9
  135.3 22.9 %collective-permute-start.10 = (bf16[2,2,128,1024]{3,2,1,0:T(8,128)(2,1)S(1)}, bf16[2,2,128,1024]{3,2,1,0:T(8,128)(2,1)S(1)}, u32[]{:S(2)}, u32[]{:S(2)}) collective-permute-start(bf16[2,2,128,1024]{3,2,1,0:T(8,128)(2,1)S(1)} %get-tuple-element.17), channel_id=1, source_target_pairs={{0,0},{1,4},{2,2},{3,6},{4,1},{5,5},{6,3},{7,7},{8,8},{9,12},{10,1... | collective-permute-start | bytes 3145736 | tf_op jit(solution)/shard_map/ppermute | solution.py:421

commit v3 on v2

--- a/solution.py
+++ b/solution.py
@@ -369,6 +369,10 @@
     xt, fwd, inv = (jnp.asarray(t) for t in tables())
 
     both = ("freq", "lat")
+    gathered = jnp.stack([m[s] for s in range(STEPS) for m in (slowness, anisotropy)])
+    gathered = lax.all_gather(gathered.astype(bf16), "freq")
+    gathered, record = lax.optimization_barrier((gathered, record))
+
     moved = lax.all_to_all(record.astype(bf16), "freq", split_axis=0, concat_axis=3, tiled=True)
     traces = receiver_cell.shape[-1]
     scalars = jnp.concatenate([frequency_index.astype(f32), wavelet.reshape(-1)])
@@ -387,8 +391,7 @@
 
     models = []
     for s in range(STEPS):
-        model = jnp.stack([slowness[s], anisotropy[s]]).astype(bf16)
-        model = lax.all_gather(model, "freq")
+        model = gathered[:, 2 * s : 2 * s + 2]
         width = model.shape[-1]
         if width != SLAB:
             model = model.transpose(1, 2, 0, 3).reshape(2, SLAB, NX // SLAB, SLAB)

time: 160 us -> 180 us (1.12)
  waiting for transfers between devices: 30 us -> 57.3 us
  blocking collectives: 39.9 us -> 20.4 us
  between operations: 2.97 us -> 16.3 us
  starting transfers between devices: 18 us -> 15 us
  other arithmetic: 3.99 us -> 6.46 us
    all_gather x0 -> x1, waiting for transfers between devices: none -> 26.3 us  [body(): gathered = lax.all_gather(gathered.astype(bf16), 'freq')]
    all_gather x2 -> x0, blocking collectives: 18.6 us -> none  [body(): model = lax.all_gather(model, 'freq')]
    another operation x4 -> x3, other arithmetic: 0.04 us -> 2.51 us
    all_to_all x1, starting transfers between devices: 5.17 us -> 3.34 us  [body(): lax.all_to_all(record.astype(bf16), 'freq', split_axis=0, concat_axis=3,...]
    unnamed x17 -> x15, local copies, waits for them, and re-layouts: 3.85 us -> 3.84 us
  transfers between devices with their start and end apart: 12 -> 13, of which waited for: 4 -> 5; matrix products, arithmetic and copies ran while one was open for 2% -> 2% of each run, Pallas kernels for 10% -> 9%
where the time goes in v3:
time: 180 us
  Pallas kernels  59.7 us (33%)
  waiting for transfers between devices  57.3 us (32%)
  blocking collectives  20.4 us (11%)
  between operations  16.3 us (9%)
  starting transfers between devices  15 us (8%)
  other arithmetic  6.46 us (4%)
  local copies, waits for them, and re-layouts  4.66 us (3%)
    all_gather x1, waiting for transfers between devices, body(): gathered = lax.all_gather(gathered.astype(bf16), 'freq')  26.3 us
    ppermute x1, waiting for transfers between devices, body(): lax.ppermute(model, both, cross)  24.6 us
    all_to_all x1, blocking collectives, body(): lax.all_to_all(images.reshape(STEPS, SLAB, nfreq, NX // nfreq).transpose(...  20.4 us
    pallas_call x2, Pallas kernels, middle(): call(functools.partial(middle_kernel, step), (HALF // width,), [pl.BlockS...  19.7 us
    pallas_call x2, Pallas kernels, inverse_x(): call(functools.partial(inverse_x_kernel, step), (NX // TILE,), [pl.BlockS...  14.9 us
    pallas_call x4, Pallas kernels, forward_x(): call(forward_x_kernel, (tiles,), [pl.BlockSpec((2, 2, rows, NX), lambda i...  13.9 us
    pallas_call x1, Pallas kernels, start_fields(): call(start_kernel, (2,), [pl.BlockSpec((1, 4, traces), lambda i, a, b: (i...  11.2 us
    ppermute x4, starting transfers between devices, body(): got = lax.ppermute(send, 'freq', pair)  5.46 us
  transfers between devices with their start and end apart: 13, of which 5 were waited for; matrix products, arithmetic and copies ran while one was open for 2% of the time, Pallas kernels for 9%

profile of v3, /device:TPU:0, one launch (start us, length us, event | category | flops | bytes accessed | tf_op | source)
XLA Modules:
  0.0 179.9 jit_solution(8391296177018525107)
XLA Ops:
  7.2 0.9 convert.19
  8.1 0.9 convert.20
  10.4 26.3 %all-gather.2.cloned.1.call-done = bf16[8,4,128,128]{3,2,1,0:T(8,128)(2,1)} async-done(((bf16[1,4,128,128]{3,2,1,0:T(8,128)(2,1)}), bf16[8,4,128,128]{3,2,1,0:T(8,128)(2,1)}) %all-gather.2.cloned.1.call-update) | async-done | bytes 1048592 | tf_op jit(solution)/shard_map/all_gather | solution.py:373
  36.7 0.8 convert_element_type.34
  38.1 3.3 %all-to-all-start = ((bf16[8,2,512]{2,1,0:T(2,128)(2,1)}), bf16[8,2,512]{2,1,0:T(2,128)(2,1)S(1)}, u32[]{:S(2)}, u32[]{:S(2)}) async-start(bf16[8,2,512]{2,1,0:T(2,128)(2,1)} %bitcast.44), calls=%async_computation | async-start | bytes 32768 | tf_op jit(solution)/shard_map/all_to_all | solution.py:376
  41.4 0.7 select_maximum_fusion
  42.8 0.7 convert_element_type.39
  43.6 2.5 %all-to-all-done = bf16[8,2,512]{2,1,0:T(2,128)(2,1)S(1)} async-done(((bf16[8,2,512]{2,1,0:T(2,128)(2,1)}), bf16[8,2,512]{2,1,0:T(2,128)(2,1)S(1)}, u32[]{:S(2)}, u32[]{:S(2)}) %all-to-all-start) | async-done | bytes 16416 | tf_op jit(solution)/shard_map/all_to_all | solution.py:376
  46.3 2.5 %collective-permute-start.1 = (f32[4,4096]{1,0:T(4,128)S(1)}, f32[4,4096]{1,0:T(4,128)S(1)}, u32[]{:S(2)}, u32[]{:S(2)}) collective-permute-start(f32[4,4096]{1,0:T(4,128)S(1)} %pad_maximum_fusion.3), channel_id=1, source_target_pairs={{0,2},{1,6},{2,0},{3,4},{4,3},{5,7},{6,1},{7,5},{8,10},{9,14},{10,... | collective-permute-start | bytes 196616 | tf_op jit(solution)/shard_map/ppermute | solution.py:387
  50.6 2.4 %collective-permute-done.1 = f32[4,4096]{1,0:T(4,128)S(1)} collective-permute-done((f32[4,4096]{1,0:T(4,128)S(1)}, f32[4,4096]{1,0:T(4,128)S(1)}, u32[]{:S(2)}, u32[]{:S(2)}) %collective-permute-start.1) | collective-permute-done | bytes 65568 | tf_op jit(solution)/shard_map/ppermute | solution.py:387
  53.1 0.7 pad_maximum_fusion.4.reals
  53.9 11.2 %shard_map.140.wave_ref = bf16[2,2,256,1024]{3,2,1,0:T(8,128)(2,1)S(1)} custom-call(s32[4]{0:T(128)S(1)} %pad_add_fusion.ints, f32[7]{0:T(128)S(1)} %pad_maximum_fusion.4.reals, f32[2,4,4096]{2,1,0:T(4,128)S(1)} %pad_maximum_fusion.2.packet_ref), custom_call_target="tpu_custom_call" | custom-call | flops 8000000000 | bytes 4194304 | tf_op jit(solution)/shard_map/pallas_call | solution.py:149
  65.1 3.5 %shard_map.142 = bf16[2,2,256,512]{3,2,1,0:T(8,128)(2,1)S(1)} custom-call(s32[4]{0:T(128)S(1)} %pad_add_fusion.ints, f32[7]{0:T(128)S(1)} %pad_maximum_fusion.4.reals, bf16[2,2,256,1024]{3,2,1,0:T(8,128)(2,1)S(1)} %shard_map.140.wave_ref, bf16[2,1024,1024]{2,1,0:T(8,128)(2,1)S(1)} %copy-done.1), custom_call_target="tpu_custom_call" | custom-call | flops 4000000000 | bytes 4194304 | tf_op jit(solution)/shard_map/pallas_call | solution.py:177
  68.6 3.5 %collective-permute-start.2 = (bf16[2,2,256,512]{3,2,1,0:T(8,128)(2,1)S(1)}, bf16[2,2,256,512]{3,2,1,0:T(8,128)(2,1)S(1)}, u32[]{:S(2)}, u32[]{:S(2)}) collective-permute-start(bf16[2,2,256,512]{3,2,1,0:T(8,128)(2,1)S(1)} %shard_map.142), channel_id=1, source_target_pairs={{0,4},{4,0},{8,12},{12,8},{16,20},{20,16},{24,28},{28,24},{1,5},{5... | collective-permute-start | bytes 3145736 | tf_op jit(solution)/shard_map/ppermute | solution.py:412
  72.1 3.5 %shard_map.141.mine_ref = bf16[2,2,256,512]{3,2,1,0:T(8,128)(2,1)S(1)} custom-call(s32[4]{0:T(128)S(1)} %pad_add_fusion.ints, f32[7]{0:T(128)S(1)} %pad_maximum_fusion.4.reals, bf16[2,2,256,1024]{3,2,1,0:T(8,128)(2,1)S(1)} %shard_map.140.wave_ref, bf16[2,1024,1024]{2,1,0:T(8,128)(2,1)S(1)} %copy-done.1), custom_call_target="tpu_custom_call" | custom-call | flops 4000000000 | bytes 4194304 | tf_op jit(solution)/shard_map/pallas_call | solution.py:177
  75.6 10.0 %shard_map.143 = (bf16[2,2,256,512]{3,2,1,0:T(8,128)(2,1)S(1)}, bf16[2,2,256,512]{3,2,1,0:T(8,128)(2,1)S(1)}) custom-call(s32[4]{0:T(128)S(1)} %pad_add_fusion.ints, f32[7]{0:T(128)S(1)} %pad_maximum_fusion.4.reals, bf16[2,2,256,512]{3,2,1,0:T(8,128)(2,1)S(1)} %shard_map.141.mine_ref, bf16[2,2,256,512]{3,2,1,0:T(8,128)(2,1)S(1)} %collective-permute-done.2.got_ref, ...), custom_call_target="tpu_custom_call" | custom-call | flops 4000000000 | bytes 4194304 | tf_op jit(solution)/shard_map/pallas_call | solution.py:234
  85.9 0.7 collective-permute-start.4
  86.6 24.6 %collective-permute-done.5.refs_1_ = bf16[8,2,128,128]{3,2,1,0:T(8,128)(2,1)S(1)} collective-permute-done((bf16[8,2,128,128]{3,2,1,0:T(8,128)(2,1)S(1)}, bf16[8,2,128,128]{3,2,1,0:T(8,128)(2,1)S(1)}, u32[]{:S(2)}, u32[]{:S(2)}) %collective-permute-start.5) | collective-permute-done | bytes 524320 | tf_op jit(solution)/shard_map/ppermute | solution.py:400
  111.2 9.4 %shard_map.144 = (bf16[2,2,256,1024]{3,2,1,0:T(8,128)(2,1)S(1)}, bf16[256,1024]{1,0:T(8,128)(2,1)S(1)}) custom-call(s32[4]{0:T(128)S(1)} %pad_add_fusion.ints, f32[7]{0:T(128)S(1)} %pad_maximum_fusion.4.reals, bf16[2,2,256,512]{3,2,1,0:T(8,128)(2,1)S(1)} %get-tuple-element.13.keep_ref, bf16[2,2,256,512]{3,2,1,0:T(8,128)(2,1)S(1)} %collective-permute-done.3.got_ref, ...), custom_call_target="tpu_custom_call" | custom-call | flops 5000000000 | bytes 4194304 | tf_op jit(solution)/shard_map/pallas_call | solution.py:310
  120.6 3.5 %shard_map.146 = bf16[2,2,256,512]{3,2,1,0:T(8,128)(2,1)S(1)} custom-call(s32[4]{0:T(128)S(1)} %pad_add_fusion.ints, f32[7]{0:T(128)S(1)} %pad_maximum_fusion.4.reals, bf16[2,2,256,1024]{3,2,1,0:T(8,128)(2,1)S(1)} %get-tuple-element.17.wave_ref, bf16[2,1024,1024]{2,1,0:T(8,128)(2,1)S(1)} %copy-done.1), custom_call_target="tpu_custom_call" | custom-call | flops 4000000000 | bytes 4194304 | tf_op jit(solution)/shard_map/pallas_call | solution.py:177
  124.1 0.9 collective-permute-start.8
  125.0 3.5 %shard_map.145.mine_ref = bf16[2,2,256,512]{3,2,1,0:T(8,128)(2,1)S(1)} custom-call(s32[4]{0:T(128)S(1)} %pad_add_fusion.ints, f32[7]{0:T(128)S(1)} %pad_maximum_fusion.4.reals, bf16[2,2,256,1024]{3,2,1,0:T(8,128)(2,1)S(1)} %get-tuple-element.17.wave_ref, bf16[2,1024,1024]{2,1,0:T(8,128)(2,1)S(1)} %copy-done.1), custom_call_target="tpu_custom_call" | custom-call | flops 4000000000 | bytes 4194304 | tf_op jit(solution)/shard_map/pallas_call | solution.py:177
  128.5 9.7 %shard_map.147 = (bf16[2,2,128,512]{3,2,1,0:T(8,128)(2,1)S(1)}, bf16[2,2,128,512]{3,2,1,0:T(8,128)(2,1)S(1)}) custom-call(s32[4]{0:T(128)S(1)} %pad_add_fusion.ints, f32[7]{0:T(128)S(1)} %pad_maximum_fusion.4.reals, bf16[2,2,256,512]{3,2,1,0:T(8,128)(2,1)S(1)} %shard_map.145.mine_ref, bf16[2,2,256,512]{3,2,1,0:T(8,128)(2,1)S(1)} %collective-permute-done.6.got_ref, ...), custom_call_target="tpu_custom_call" | custom-call | flops 4000000000 | bytes 4194304 | tf_op jit(solution)/shard_map/pallas_call | solution.py:234
  138.3 1.8 collective-permute-start.7
  140.1 1.5 collective-permute-done.7.got_ref
  141.6 2.2 %copy-done.2 = bf16[2,1024,1024]{2,1,0:T(8,128)(2,1)S(1)} copy-done((bf16[2,1024,1024]{2,1,0:T(8,128)(2,1)S(1)}, bf16[2,1024,1024]{2,1,0:T(8,128)(2,1)}, u32[]{:S(2)}) %copy-start.2) | copy-done | bytes 4194328
  143.7 5.5 %shard_map.148 = (bf16[2,2,128,1024]{3,2,1,0:T(8,128)(2,1)S(1)}, bf16[128,1024]{1,0:T(8,128)(2,1)S(1)}) custom-call(s32[4]{0:T(128)S(1)} %pad_add_fusion.ints, f32[7]{0:T(128)S(1)} %pad_maximum_fusion.4.reals, bf16[2,2,128,512]{3,2,1,0:T(8,128)(2,1)S(1)} %get-tuple-element.18.keep_ref, bf16[2,2,128,512]{3,2,1,0:T(8,128)(2,1)S(1)} %collective-permute-done.7.got_ref, ...), custom_call_target="tpu_custom_call" | custom-call | flops 5000000000 | bytes 4194304 | tf_op jit(solution)/shard_map/pallas_call | solution.py:310
  149.3 0.7 collective-permute-start.9
  150.0 0.7 collective-permute-start.10
  150.9 20.4 %all_to_all.14 = bf16[8,2,128,128]{3,2,1,0:T(8,128)(2,1)S(1)} all-to-all(bf16[8,2,128,128]{3,2,1,0:T(8,128)(2,1)S(1)} %bitcast_bitcast_fusion), channel_id=1, replica_groups=mesh['freq'=8,'lat'=4] {'freq'}, dimensions={0} | all-to-all | bytes 1048576 | tf_op jit(solution)/shard_map/all_to_all | solution.py:421
  171.3 0.7 convert_reduce_fusion
  172.0 1.0 copy.29
  (40 shorter events, 3.4 us)
Async XLA Ops:
  7.2 29.5 %all-gather.2.cloned.1.call-start = ((), (), s32[]{:S(2)}) async-start(), calls=%async_computation.2 | async-start | bytes 1179648 | tf_op jit(solution)/shard_map/all_gather | solution.py:373
  38.1 8.0 %all-to-all-start = ((bf16[8,2,512]{2,1,0:T(2,128)(2,1)}), bf16[8,2,512]{2,1,0:T(2,128)(2,1)S(1)}, u32[]{:S(2)}, u32[]{:S(2)}) async-start(bf16[8,2,512]{2,1,0:T(2,128)(2,1)} %bitcast.44), calls=%async_computation | async-start | bytes 32768 | tf_op jit(solution)/shard_map/all_to_all | solution.py:376
  46.3 6.8 %collective-permute-start.1 = (f32[4,4096]{1,0:T(4,128)S(1)}, f32[4,4096]{1,0:T(4,128)S(1)}, u32[]{:S(2)}, u32[]{:S(2)}) collective-permute-start(f32[4,4096]{1,0:T(4,128)S(1)} %pad_maximum_fusion.3), channel_id=1, source_target_pairs={{0,2},{1,6},{2,0},{3,4},{4,3},{5,7},{6,1},{7,5},{8,10},{9,14},{10,... | collective-permute-start | bytes 196616 | tf_op jit(solution)/shard_map/ppermute | solution.py:387
  48.7 0.7 collective-permute-start
  53.9 11.2 %copy-start.1 = (bf16[2,1024,1024]{2,1,0:T(8,128)(2,1)S(1)}, bf16[2,1024,1024]{2,1,0:T(8,128)(2,1)}, u32[]{:S(2)}) copy-start(bf16[2,1024,1024]{2,1,0:T(8,128)(2,1)} %constant.62.clone.table_ref.tm_ref.tg_ref) | copy-start | bytes 12582916
  68.6 7.0 %copy-start.3 = (bf16[2,2,256,1024]{3,2,1,0:T(8,128)(2,1)S(1)}, bf16[2,2,256,1024]{3,2,1,0:T(8,128)(2,1)}, u32[]{:S(2)}) copy-start(bf16[2,2,256,1024]{3,2,1,0:T(8,128)(2,1)} %constant.64.clone.im_ref.ig_ref) | copy-start | bytes 6291460
  68.6 7.0 %copy-start.4 = (bf16[2,1024,512]{2,1,0:T(8,128)(2,1)S(1)}, bf16[2,1024,512]{2,1,0:T(8,128)(2,1)}, u32[]{:S(2)}) copy-start(bf16[2,1024,512]{2,1,0:T(8,128)(2,1)} %constant.63.clone.fm_ref.fg_ref) | copy-start | bytes 6291460
  68.6 7.0 %collective-permute-start.2 = (bf16[2,2,256,512]{3,2,1,0:T(8,128)(2,1)S(1)}, bf16[2,2,256,512]{3,2,1,0:T(8,128)(2,1)S(1)}, u32[]{:S(2)}, u32[]{:S(2)}) collective-permute-start(bf16[2,2,256,512]{3,2,1,0:T(8,128)(2,1)S(1)} %shard_map.142), channel_id=1, source_target_pairs={{0,4},{4,0},{8,12},{12,8},{16,20},{20,16},{24,28},{28,24},{1,5},{5... | collective-permute-start | bytes 3145736 | tf_op jit(solution)/shard_map/ppermute | solution.py:412
  75.6 10.1 %copy-start.5 = (bf16[8,4,128,128]{3,2,1,0:T(8,128)(2,1)S(1)}, bf16[8,4,128,128]{3,2,1,0:T(8,128)(2,1)}, u32[]{:S(2)}) copy-start(bf16[8,4,128,128]{3,2,1,0:T(8,128)(2,1)} %all-gather.2.cloned.1.call-done) | copy-start | bytes 3145732
  85.6 25.5 %copy-start = (bf16[2,128,128]{2,1,0:T(8,128)(2,1)S(1)}, bf16[2,128,128]{2,1,0:T(8,128)(2,1)}, u32[]{:S(2)}) copy-start(bf16[2,128,128]{2,1,0:T(8,128)(2,1)} %refs_1_.1) | copy-start | bytes 196612
  85.6 25.5 %collective-permute-start.3 = (bf16[2,2,256,512]{3,2,1,0:T(8,128)(2,1)S(1)}, bf16[2,2,256,512]{3,2,1,0:T(8,128)(2,1)S(1)}, u32[]{:S(2)}, u32[]{:S(2)}) collective-permute-start(bf16[2,2,256,512]{3,2,1,0:T(8,128)(2,1)S(1)} %get-tuple-element.14), channel_id=1, source_target_pairs={{0,4},{4,0},{8,12},{12,8},{16,20},{20,16},{24,28},{28,24},{1,5},{5... | collective-permute-start | bytes 3145736 | tf_op jit(solution)/shard_map/ppermute | solution.py:415
  85.8 25.4 %collective-permute-start.5 = (bf16[8,2,128,128]{3,2,1,0:T(8,128)(2,1)S(1)}, bf16[8,2,128,128]{3,2,1,0:T(8,128)(2,1)S(1)}, u32[]{:S(2)}, u32[]{:S(2)}) collective-permute-start(bf16[8,2,128,128]{3,2,1,0:T(8,128)(2,1)S(1)} %get-tuple-element.27), channel_id=1, source_target_pairs={{0,2},{1,6},{2,0},{3,4},{4,3},{5,7},{6,1},{7,5},{8,10},{9,14},{10,... | collective-permute-start | bytes 1572872 | tf_op jit(solution)/shard_map/ppermute | solution.py:400
  85.9 25.3 %collective-permute-start.4 = (bf16[8,2,128,128]{3,2,1,0:T(8,128)(2,1)S(1)}, bf16[8,2,128,128]{3,2,1,0:T(8,128)(2,1)S(1)}, u32[]{:S(2)}, u32[]{:S(2)}) collective-permute-start(bf16[8,2,128,128]{3,2,1,0:T(8,128)(2,1)S(1)} %get-tuple-element.27), channel_id=1, source_target_pairs={{0,0},{1,4},{2,2},{3,6},{4,1},{5,5},{6,3},{7,7},{8,8},{9,12},{10,1... | collective-permute-start | bytes 1572872 | tf_op jit(solution)/shard_map/ppermute | solution.py:399
  124.1 4.4 %collective-permute-start.6 = (bf16[2,2,256,512]{3,2,1,0:T(8,128)(2,1)S(1)}, bf16[2,2,256,512]{3,2,1,0:T(8,128)(2,1)S(1)}, u32[]{:S(2)}, u32[]{:S(2)}) collective-permute-start(bf16[2,2,256,512]{3,2,1,0:T(8,128)(2,1)S(1)} %shard_map.146), channel_id=1, source_target_pairs={{0,4},{4,0},{8,12},{12,8},{16,20},{20,16},{24,28},{28,24},{1,5},{5... | collective-permute-start | bytes 3145736 | tf_op jit(solution)/shard_map/ppermute | solution.py:412
  124.1 15.9 %collective-permute-start.8 = (bf16[8,2,128,128]{3,2,1,0:T(8,128)(2,1)S(1)}, bf16[8,2,128,128]{3,2,1,0:T(8,128)(2,1)S(1)}, u32[]{:S(2)}, u32[]{:S(2)}) collective-permute-start(bf16[8,2,128,128]{3,2,1,0:T(8,128)(2,1)S(1)} %get-tuple-element.26), channel_id=1, source_target_pairs={{0,0},{1,4},{2,2},{3,6},{4,1},{5,5},{6,3},{7,7},{8,8},{9,12},{10,1... | collective-permute-start | bytes 1572872 | tf_op jit(solution)/shard_map/ppermute | solution.py:399
  138.3 3.3 %collective-permute-start.7 = (bf16[2,2,128,512]{3,2,1,0:T(8,128)(2,1)S(1)}, bf16[2,2,128,512]{3,2,1,0:T(8,128)(2,1)S(1)}, u32[]{:S(2)}, u32[]{:S(2)}) collective-permute-start(bf16[2,2,128,512]{3,2,1,0:T(8,128)(2,1)S(1)} %get-tuple-element.19), channel_id=1, source_target_pairs={{0,4},{4,0},{8,12},{12,8},{16,20},{20,16},{24,28},{28,24},{1,5},{5... | collective-permute-start | bytes 1572872 | tf_op jit(solution)/shard_map/ppermute | solution.py:415
  141.6 2.2 %copy-start.2 = (bf16[2,1024,1024]{2,1,0:T(8,128)(2,1)S(1)}, bf16[2,1024,1024]{2,1,0:T(8,128)(2,1)}, u32[]{:S(2)}) copy-start(bf16[2,1024,1024]{2,1,0:T(8,128)(2,1)} %constant.62.clone.table_ref.tm_ref.tg_ref) | copy-start | bytes 12582916
  149.3 1.4 collective-permute-start.9
  150.0 22.0 %collective-permute-start.10 = (bf16[2,2,128,1024]{3,2,1,0:T(8,128)(2,1)S(1)}, bf16[2,2,128,1024]{3,2,1,0:T(8,128)(2,1)S(1)}, u32[]{:S(2)}, u32[]{:S(2)}) collective-permute-start(bf16[2,2,128,1024]{3,2,1,0:T(8,128)(2,1)S(1)} %get-tuple-element.21), channel_id=1, source_target_pairs={{0,0},{1,4},{2,2},{3,6},{4,1},{5,5},{6,3},{7,7},{8,8},{9,12},{10,1... | collective-permute-start | bytes 3145736 | tf_op jit(solution)/shard_map/ppermute | solution.py:424
Sparse Core Ops, SparseCore 0:
  10.5 26.1 all-gather.1

commit v4 on v2

--- a/solution.py
+++ b/solution.py
@@ -389,6 +389,8 @@
     for s in range(STEPS):
         model = jnp.stack([slowness[s], anisotropy[s]]).astype(bf16)
         model = lax.all_gather(model, "freq")
+        if s == 0:
+            model, packets = lax.optimization_barrier((model, packets))
         width = model.shape[-1]
         if width != SLAB:
             model = model.transpose(1, 2, 0, 3).reshape(2, SLAB, NX // SLAB, SLAB)

time: 160 us -> 162 us (1.012)
    all_to_all x1, waiting for transfers between devices: 1.93 us -> 0.01 us  [body(): lax.all_to_all(record.astype(bf16), 'freq', split_axis=0, concat_axis=3,...]
    another operation x2, other arithmetic: 0.02 us -> 1.83 us
  transfers between devices with their start and end apart: 12 -> 12, of which waited for: 4 -> 3; matrix products, arithmetic and copies ran while one was open for 2% -> 3% of each run, Pallas kernels for 10% -> 10%
where the time goes in v4:
time: 162 us; the launch traced here: 161 us
  Pallas kernels  59.6 us (37%)
  blocking collectives  41.5 us (26%)
  waiting for transfers between devices  29.4 us (18%)
  starting transfers between devices  17.8 us (11%)
  other arithmetic  5.14 us (3%)
  local copies, waits for them, and re-layouts  4.59 us (3%)
  between operations  2.96 us (2%)
    ppermute x1, waiting for transfers between devices, body(): lax.ppermute(model, both, cross)  24.7 us
    all_to_all x1, blocking collectives, body(): lax.all_to_all(images.reshape(STEPS, SLAB, nfreq, NX // nfreq).transpose(...  21.3 us
    all_gather x2, blocking collectives, body(): model = lax.all_gather(model, 'freq')  20.2 us
    pallas_call x2, Pallas kernels, middle(): call(functools.partial(middle_kernel, step), (HALF // width,), [pl.BlockS...  19.7 us
    pallas_call x2, Pallas kernels, inverse_x(): call(functools.partial(inverse_x_kernel, step), (NX // TILE,), [pl.BlockS...  14.9 us
    pallas_call x4, Pallas kernels, forward_x(): call(forward_x_kernel, (tiles,), [pl.BlockSpec((2, 2, rows, NX), lambda i...  13.8 us
    pallas_call x1, Pallas kernels, start_fields(): call(start_kernel, (2,), [pl.BlockSpec((1, 4, traces), lambda i, a, b: (i...  11.2 us
    all_to_all x1, starting transfers between devices, body(): lax.all_to_all(record.astype(bf16), 'freq', split_axis=0, concat_axis=3,...  5.17 us
  transfers between devices with their start and end apart: 12, of which 3 were waited for; matrix products, arithmetic and copies ran while one was open for 3% of the time, Pallas kernels for 10%

profile of v4, /device:TPU:0, one launch (start us, length us, event | category | flops | bytes accessed | tf_op | source)
XLA Modules:
  0.0 161.1 jit_solution(4550613908961561335)
XLA Ops:
  0.6 0.8 convert_element_type.42
  2.1 5.2 %all-to-all-start = ((bf16[8,2,512]{2,1,0:T(2,128)(2,1)}), bf16[8,2,512]{2,1,0:T(2,128)(2,1)S(1)}, u32[]{:S(2)}, u32[]{:S(2)}) async-start(bf16[8,2,512]{2,1,0:T(2,128)(2,1)} %bitcast.44), calls=%async_computation | async-start | bytes 32768 | tf_op jit(solution)/shard_map/all_to_all | solution.py:372
  7.9 0.9 convert.19
  8.8 0.9 convert.20
  9.8 10.4 %all_gather.8 = bf16[8,2,128,128]{3,2,1,0:T(8,128)(2,1)S(1)} all-gather(bf16[1,2,128,128]{3,2,1,0:T(8,128)(2,1)S(1)} %pad_maximum_fusion.3), channel_id=1, replica_groups=mesh['freq'=8,'lat'=4] {'freq'}, dimensions={0}, use_global_device_ids=true | all-gather | bytes 589824 | tf_op jit(solution)/shard_map/all_gather | solution.py:391
  20.1 0.7 select_maximum_fusion
  21.5 0.7 convert_element_type.47
  23.1 2.7 %collective-permute-start.1 = (f32[4,4096]{1,0:T(4,128)S(1)}, f32[4,4096]{1,0:T(4,128)S(1)}, u32[]{:S(2)}, u32[]{:S(2)}) collective-permute-start(f32[4,4096]{1,0:T(4,128)S(1)} %pad_maximum_fusion.2), channel_id=1, source_target_pairs={{0,2},{1,6},{2,0},{3,4},{4,3},{5,7},{6,1},{7,5},{8,10},{9,14},{10,... | collective-permute-start | bytes 196616 | tf_op jit(solution)/shard_map/ppermute | solution.py:383
  25.9 3.2 %collective-permute-done.1 = f32[4,4096]{1,0:T(4,128)S(1)} collective-permute-done((f32[4,4096]{1,0:T(4,128)S(1)}, f32[4,4096]{1,0:T(4,128)S(1)}, u32[]{:S(2)}, u32[]{:S(2)}) %collective-permute-start.1) | collective-permute-done | bytes 65568 | tf_op jit(solution)/shard_map/ppermute | solution.py:383
  30.4 11.2 %shard_map.140.wave_ref = bf16[2,2,256,1024]{3,2,1,0:T(8,128)(2,1)S(1)} custom-call(s32[4]{0:T(128)S(1)} %pad_add_fusion.ints, f32[7]{0:T(128)S(1)} %pad_maximum_fusion.5.reals, f32[2,4,4096]{2,1,0:T(4,128)S(1)} %pad_maximum_fusion.1.packet_ref), custom_call_target="tpu_custom_call" | custom-call | flops 8000000000 | bytes 4194304 | tf_op jit(solution)/shard_map/pallas_call | solution.py:149
  41.6 3.5 %shard_map.142 = bf16[2,2,256,512]{3,2,1,0:T(8,128)(2,1)S(1)} custom-call(s32[4]{0:T(128)S(1)} %pad_add_fusion.ints, f32[7]{0:T(128)S(1)} %pad_maximum_fusion.5.reals, bf16[2,2,256,1024]{3,2,1,0:T(8,128)(2,1)S(1)} %shard_map.140.wave_ref, bf16[2,1024,1024]{2,1,0:T(8,128)(2,1)S(1)} %copy-done.1), custom_call_target="tpu_custom_call" | custom-call | flops 4000000000 | bytes 4194304 | tf_op jit(solution)/shard_map/pallas_call | solution.py:177
  45.2 2.6 %collective-permute-start.2 = (bf16[2,2,256,512]{3,2,1,0:T(8,128)(2,1)S(1)}, bf16[2,2,256,512]{3,2,1,0:T(8,128)(2,1)S(1)}, u32[]{:S(2)}, u32[]{:S(2)}) collective-permute-start(bf16[2,2,256,512]{3,2,1,0:T(8,128)(2,1)S(1)} %shard_map.142), channel_id=1, source_target_pairs={{0,4},{4,0},{8,12},{12,8},{16,20},{20,16},{24,28},{28,24},{1,5},{5... | collective-permute-start | bytes 3145736 | tf_op jit(solution)/shard_map/ppermute | solution.py:411
  47.8 3.5 %shard_map.141.mine_ref = bf16[2,2,256,512]{3,2,1,0:T(8,128)(2,1)S(1)} custom-call(s32[4]{0:T(128)S(1)} %pad_add_fusion.ints, f32[7]{0:T(128)S(1)} %pad_maximum_fusion.5.reals, bf16[2,2,256,1024]{3,2,1,0:T(8,128)(2,1)S(1)} %shard_map.140.wave_ref, bf16[2,1024,1024]{2,1,0:T(8,128)(2,1)S(1)} %copy-done.1), custom_call_target="tpu_custom_call" | custom-call | flops 4000000000 | bytes 4194304 | tf_op jit(solution)/shard_map/pallas_call | solution.py:177
  51.3 10.0 %shard_map.143 = (bf16[2,2,256,512]{3,2,1,0:T(8,128)(2,1)S(1)}, bf16[2,2,256,512]{3,2,1,0:T(8,128)(2,1)S(1)}) custom-call(s32[4]{0:T(128)S(1)} %pad_add_fusion.ints, f32[7]{0:T(128)S(1)} %pad_maximum_fusion.5.reals, bf16[2,2,256,512]{3,2,1,0:T(8,128)(2,1)S(1)} %shard_map.141.mine_ref, bf16[2,2,256,512]{3,2,1,0:T(8,128)(2,1)S(1)} %collective-permute-done.2.got_ref, ...), custom_call_target="tpu_custom_call" | custom-call | flops 4000000000 | bytes 4194304 | tf_op jit(solution)/shard_map/pallas_call | solution.py:234
  61.3 0.7 collective-permute-start.4
  62.0 1.6 collective-permute-start.5
  63.6 24.7 %collective-permute-done.5.refs_1_ = bf16[8,2,128,128]{3,2,1,0:T(8,128)(2,1)S(1)} collective-permute-done((bf16[8,2,128,128]{3,2,1,0:T(8,128)(2,1)S(1)}, bf16[8,2,128,128]{3,2,1,0:T(8,128)(2,1)S(1)}, u32[]{:S(2)}, u32[]{:S(2)}) %collective-permute-start.5) | collective-permute-done | bytes 524320 | tf_op jit(solution)/shard_map/ppermute | solution.py:399
  88.3 9.4 %shard_map.144 = (bf16[2,2,256,1024]{3,2,1,0:T(8,128)(2,1)S(1)}, bf16[256,1024]{1,0:T(8,128)(2,1)S(1)}) custom-call(s32[4]{0:T(128)S(1)} %pad_add_fusion.ints, f32[7]{0:T(128)S(1)} %pad_maximum_fusion.5.reals, bf16[2,2,256,512]{3,2,1,0:T(8,128)(2,1)S(1)} %get-tuple-element.13.keep_ref, bf16[2,2,256,512]{3,2,1,0:T(8,128)(2,1)S(1)} %collective-permute-done.3.got_ref, ...), custom_call_target="tpu_custom_call" | custom-call | flops 5000000000 | bytes 4194304 | tf_op jit(solution)/shard_map/pallas_call | solution.py:310
  97.7 3.5 %shard_map.146 = bf16[2,2,256,512]{3,2,1,0:T(8,128)(2,1)S(1)} custom-call(s32[4]{0:T(128)S(1)} %pad_add_fusion.ints, f32[7]{0:T(128)S(1)} %pad_maximum_fusion.5.reals, bf16[2,2,256,1024]{3,2,1,0:T(8,128)(2,1)S(1)} %get-tuple-element.17.wave_ref, bf16[2,1024,1024]{2,1,0:T(8,128)(2,1)S(1)} %copy-done.1), custom_call_target="tpu_custom_call" | custom-call | flops 4000000000 | bytes 4194304 | tf_op jit(solution)/shard_map/pallas_call | solution.py:177
  101.2 9.8 %all_gather.9 = bf16[8,2,128,128]{3,2,1,0:T(8,128)(2,1)S(1)} all-gather(bf16[1,2,128,128]{3,2,1,0:T(8,128)(2,1)S(1)} %pad_maximum_fusion.4), channel_id=1, replica_groups=mesh['freq'=8,'lat'=4] {'freq'}, dimensions={0}, use_global_device_ids=true | all-gather | bytes 589824 | tf_op jit(solution)/shard_map/all_gather | solution.py:391
  111.1 0.9 collective-permute-start.8
  112.0 3.5 %shard_map.145.mine_ref = bf16[2,2,256,512]{3,2,1,0:T(8,128)(2,1)S(1)} custom-call(s32[4]{0:T(128)S(1)} %pad_add_fusion.ints, f32[7]{0:T(128)S(1)} %pad_maximum_fusion.5.reals, bf16[2,2,256,1024]{3,2,1,0:T(8,128)(2,1)S(1)} %get-tuple-element.17.wave_ref, bf16[2,1024,1024]{2,1,0:T(8,128)(2,1)S(1)} %copy-done.1), custom_call_target="tpu_custom_call" | custom-call | flops 4000000000 | bytes 4194304 | tf_op jit(solution)/shard_map/pallas_call | solution.py:177
  115.4 9.7 %shard_map.147 = (bf16[2,2,128,512]{3,2,1,0:T(8,128)(2,1)S(1)}, bf16[2,2,128,512]{3,2,1,0:T(8,128)(2,1)S(1)}) custom-call(s32[4]{0:T(128)S(1)} %pad_add_fusion.ints, f32[7]{0:T(128)S(1)} %pad_maximum_fusion.5.reals, bf16[2,2,256,512]{3,2,1,0:T(8,128)(2,1)S(1)} %shard_map.145.mine_ref, bf16[2,2,256,512]{3,2,1,0:T(8,128)(2,1)S(1)} %collective-permute-done.6.got_ref, ...), custom_call_target="tpu_custom_call" | custom-call | flops 4000000000 | bytes 4194304 | tf_op jit(solution)/shard_map/pallas_call | solution.py:234
  125.2 2.0 %collective-permute-start.7 = (bf16[2,2,128,512]{3,2,1,0:T(8,128)(2,1)S(1)}, bf16[2,2,128,512]{3,2,1,0:T(8,128)(2,1)S(1)}, u32[]{:S(2)}, u32[]{:S(2)}) collective-permute-start(bf16[2,2,128,512]{3,2,1,0:T(8,128)(2,1)S(1)} %get-tuple-element.19), channel_id=1, source_target_pairs={{0,4},{4,0},{8,12},{12,8},{16,20},{20,16},{24,28},{28,24},{1,5},{5... | collective-permute-start | bytes 1572872 | tf_op jit(solution)/shard_map/ppermute | solution.py:414
  127.2 1.5 collective-permute-done.7.got_ref
  128.7 2.2 %copy-done.2 = bf16[2,1024,1024]{2,1,0:T(8,128)(2,1)S(1)} copy-done((bf16[2,1024,1024]{2,1,0:T(8,128)(2,1)S(1)}, bf16[2,1024,1024]{2,1,0:T(8,128)(2,1)}, u32[]{:S(2)}) %copy-start.2) | copy-done | bytes 4194328
  130.9 5.5 %shard_map.148 = (bf16[2,2,128,1024]{3,2,1,0:T(8,128)(2,1)S(1)}, bf16[128,1024]{1,0:T(8,128)(2,1)S(1)}) custom-call(s32[4]{0:T(128)S(1)} %pad_add_fusion.ints, f32[7]{0:T(128)S(1)} %pad_maximum_fusion.5.reals, bf16[2,2,128,512]{3,2,1,0:T(8,128)(2,1)S(1)} %get-tuple-element.18.keep_ref, bf16[2,2,128,512]{3,2,1,0:T(8,128)(2,1)S(1)} %collective-permute-done.7.got_ref, ...), custom_call_target="tpu_custom_call" | custom-call | flops 5000000000 | bytes 4194304 | tf_op jit(solution)/shard_map/pallas_call | solution.py:310
  136.5 0.7 collective-permute-start.9
  137.2 0.7 collective-permute-start.10
  138.1 21.3 %all_to_all.14 = bf16[8,2,128,128]{3,2,1,0:T(8,128)(2,1)S(1)} all-to-all(bf16[8,2,128,128]{3,2,1,0:T(8,128)(2,1)S(1)} %bitcast_bitcast_fusion), channel_id=1, replica_groups=mesh['freq'=8,'lat'=4] {'freq'}, dimensions={0} | all-to-all | bytes 1048576 | tf_op jit(solution)/shard_map/all_to_all | solution.py:420
  159.4 0.7 convert_reduce_fusion
  160.1 1.0 copy.29
  (41 shorter events, 2.6 us)
Async XLA Ops:
  0.6 29.7 %copy-start.6 = (f32[2]{0:T(128)S(1)}, f32[2]{0:T(128)}, u32[]{:S(2)}) copy-start(f32[2]{0:T(128)} %param.20) | copy-start | bytes 28
  0.6 29.7 %copy-start.5 = (f32[2]{0:T(128)S(1)}, f32[2]{0:T(128)}, u32[]{:S(2)}) copy-start(f32[2]{0:T(128)} %param.21) | copy-start | bytes 28
  2.1 20.2 %all-to-all-start = ((bf16[8,2,512]{2,1,0:T(2,128)(2,1)}), bf16[8,2,512]{2,1,0:T(2,128)(2,1)S(1)}, u32[]{:S(2)}, u32[]{:S(2)}) async-start(bf16[8,2,512]{2,1,0:T(2,128)(2,1)} %bitcast.44), calls=%async_computation | async-start | bytes 32768 | tf_op jit(solution)/shard_map/all_to_all | solution.py:372
  22.5 3.4 %collective-permute-start = (f32[4,4096]{1,0:T(4,128)S(1)}, f32[4,4096]{1,0:T(4,128)S(1)}, u32[]{:S(2)}, u32[]{:S(2)}) collective-permute-start(f32[4,4096]{1,0:T(4,128)S(1)} %pad_maximum_fusion.2), channel_id=1, source_target_pairs={{0,0},{1,4},{2,2},{3,6},{4,1},{5,5},{6,3},{7,7},{8,8},{9,12},{10,1... | collective-permute-start | bytes 196616 | tf_op jit(solution)/shard_map/ppermute | solution.py:382
  23.1 5.9 %collective-permute-start.1 = (f32[4,4096]{1,0:T(4,128)S(1)}, f32[4,4096]{1,0:T(4,128)S(1)}, u32[]{:S(2)}, u32[]{:S(2)}) collective-permute-start(f32[4,4096]{1,0:T(4,128)S(1)} %pad_maximum_fusion.2), channel_id=1, source_target_pairs={{0,2},{1,6},{2,0},{3,4},{4,3},{5,7},{6,1},{7,5},{8,10},{9,14},{10,... | collective-permute-start | bytes 196616 | tf_op jit(solution)/shard_map/ppermute | solution.py:383
  30.4 11.2 %copy-start.1 = (bf16[2,1024,1024]{2,1,0:T(8,128)(2,1)S(1)}, bf16[2,1024,1024]{2,1,0:T(8,128)(2,1)}, u32[]{:S(2)}) copy-start(bf16[2,1024,1024]{2,1,0:T(8,128)(2,1)} %constant.62.clone.table_ref.tm_ref.tg_ref) | copy-start | bytes 12582916
  45.1 6.1 %copy-start.3 = (bf16[2,1024,512]{2,1,0:T(8,128)(2,1)S(1)}, bf16[2,1024,512]{2,1,0:T(8,128)(2,1)}, u32[]{:S(2)}) copy-start(bf16[2,1024,512]{2,1,0:T(8,128)(2,1)} %constant.63.clone.fm_ref.fg_ref) | copy-start | bytes 6291460
  45.1 6.1 %copy-start.4 = (bf16[2,2,256,1024]{3,2,1,0:T(8,128)(2,1)S(1)}, bf16[2,2,256,1024]{3,2,1,0:T(8,128)(2,1)}, u32[]{:S(2)}) copy-start(bf16[2,2,256,1024]{3,2,1,0:T(8,128)(2,1)} %constant.64.clone.im_ref.ig_ref) | copy-start | bytes 6291460
  45.2 6.1 %collective-permute-start.2 = (bf16[2,2,256,512]{3,2,1,0:T(8,128)(2,1)S(1)}, bf16[2,2,256,512]{3,2,1,0:T(8,128)(2,1)S(1)}, u32[]{:S(2)}, u32[]{:S(2)}) collective-permute-start(bf16[2,2,256,512]{3,2,1,0:T(8,128)(2,1)S(1)} %shard_map.142), channel_id=1, source_target_pairs={{0,4},{4,0},{8,12},{12,8},{16,20},{20,16},{24,28},{28,24},{1,5},{5... | collective-permute-start | bytes 3145736 | tf_op jit(solution)/shard_map/ppermute | solution.py:411
  51.2 37.0 %copy-start = (bf16[2,128,128]{2,1,0:T(8,128)(2,1)S(1)}, bf16[2,128,128]{2,1,0:T(8,128)(2,1)}, u32[]{:S(2)}) copy-start(bf16[2,128,128]{2,1,0:T(8,128)(2,1)} %refs_1_.1) | copy-start | bytes 196612
  61.3 27.0 %collective-permute-start.3 = (bf16[2,2,256,512]{3,2,1,0:T(8,128)(2,1)S(1)}, bf16[2,2,256,512]{3,2,1,0:T(8,128)(2,1)S(1)}, u32[]{:S(2)}, u32[]{:S(2)}) collective-permute-start(bf16[2,2,256,512]{3,2,1,0:T(8,128)(2,1)S(1)} %get-tuple-element.14), channel_id=1, source_target_pairs={{0,4},{4,0},{8,12},{12,8},{16,20},{20,16},{24,28},{28,24},{1,5},{5... | collective-permute-start | bytes 3145736 | tf_op jit(solution)/shard_map/ppermute | solution.py:414
  61.3 2.3 %collective-permute-start.4 = (bf16[8,2,128,128]{3,2,1,0:T(8,128)(2,1)S(1)}, bf16[8,2,128,128]{3,2,1,0:T(8,128)(2,1)S(1)}, u32[]{:S(2)}, u32[]{:S(2)}) collective-permute-start(bf16[8,2,128,128]{3,2,1,0:T(8,128)(2,1)S(1)} %all_gather.8), channel_id=1, source_target_pairs={{0,0},{1,4},{2,2},{3,6},{4,1},{5,5},{6,3},{7,7},{8,8},{9,12},{10,1... | collective-permute-start | bytes 1572872 | tf_op jit(solution)/shard_map/ppermute | solution.py:398
  62.0 26.2 %collective-permute-start.5 = (bf16[8,2,128,128]{3,2,1,0:T(8,128)(2,1)S(1)}, bf16[8,2,128,128]{3,2,1,0:T(8,128)(2,1)S(1)}, u32[]{:S(2)}, u32[]{:S(2)}) collective-permute-start(bf16[8,2,128,128]{3,2,1,0:T(8,128)(2,1)S(1)} %all_gather.8), channel_id=1, source_target_pairs={{0,2},{1,6},{2,0},{3,4},{4,3},{5,7},{6,1},{7,5},{8,10},{9,14},{10,... | collective-permute-start | bytes 1572872 | tf_op jit(solution)/shard_map/ppermute | solution.py:399
  101.1 14.3 %collective-permute-start.6 = (bf16[2,2,256,512]{3,2,1,0:T(8,128)(2,1)S(1)}, bf16[2,2,256,512]{3,2,1,0:T(8,128)(2,1)S(1)}, u32[]{:S(2)}, u32[]{:S(2)}) collective-permute-start(bf16[2,2,256,512]{3,2,1,0:T(8,128)(2,1)S(1)} %shard_map.146), channel_id=1, source_target_pairs={{0,4},{4,0},{8,12},{12,8},{16,20},{20,16},{24,28},{28,24},{1,5},{5... | collective-permute-start | bytes 3145736 | tf_op jit(solution)/shard_map/ppermute | solution.py:411
  111.1 16.1 %collective-permute-start.8 = (bf16[8,2,128,128]{3,2,1,0:T(8,128)(2,1)S(1)}, bf16[8,2,128,128]{3,2,1,0:T(8,128)(2,1)S(1)}, u32[]{:S(2)}, u32[]{:S(2)}) collective-permute-start(bf16[8,2,128,128]{3,2,1,0:T(8,128)(2,1)S(1)} %all_gather.9), channel_id=1, source_target_pairs={{0,0},{1,4},{2,2},{3,6},{4,1},{5,5},{6,3},{7,7},{8,8},{9,12},{10,1... | collective-permute-start | bytes 1572872 | tf_op jit(solution)/shard_map/ppermute | solution.py:398
  125.2 3.6 %collective-permute-start.7 = (bf16[2,2,128,512]{3,2,1,0:T(8,128)(2,1)S(1)}, bf16[2,2,128,512]{3,2,1,0:T(8,128)(2,1)S(1)}, u32[]{:S(2)}, u32[]{:S(2)}) collective-permute-start(bf16[2,2,128,512]{3,2,1,0:T(8,128)(2,1)S(1)} %get-tuple-element.19), channel_id=1, source_target_pairs={{0,4},{4,0},{8,12},{12,8},{16,20},{20,16},{24,28},{28,24},{1,5},{5... | collective-permute-start | bytes 1572872 | tf_op jit(solution)/shard_map/ppermute | solution.py:414
  128.7 2.2 %copy-start.2 = (bf16[2,1024,1024]{2,1,0:T(8,128)(2,1)S(1)}, bf16[2,1024,1024]{2,1,0:T(8,128)(2,1)}, u32[]{:S(2)}) copy-start(bf16[2,1024,1024]{2,1,0:T(8,128)(2,1)} %constant.62.clone.table_ref.tm_ref.tg_ref) | copy-start | bytes 12582916
  136.5 1.4 collective-permute-start.9
  137.2 22.9 %collective-permute-start.10 = (bf16[2,2,128,1024]{3,2,1,0:T(8,128)(2,1)S(1)}, bf16[2,2,128,1024]{3,2,1,0:T(8,128)(2,1)S(1)}, u32[]{:S(2)}, u32[]{:S(2)}) collective-permute-start(bf16[2,2,128,1024]{3,2,1,0:T(8,128)(2,1)S(1)} %get-tuple-element.21), channel_id=1, source_target_pairs={{0,0},{1,4},{2,2},{3,6},{4,1},{5,5},{6,3},{7,7},{8,8},{9,12},{10,1... | collective-permute-start | bytes 3145736 | tf_op jit(solution)/shard_map/ppermute | solution.py:423
